TPU v7x, 512 devices: a whole 4x8x8 slice. The times are simulated.
512 devices in a mesh: replica: 32 (over y_lo, z, core), tensor: 16 (over y_hi, x).
Axes of the slice: x: 4, y: 8 (y_hi: 4, y_lo: 2; y = y_hi * 2 + y_lo), z: 8, core: 2. Of those that a mesh axis runs over, the one named last changes fastest.
Arguments:
- span_query: bfloat16 [8192, 8192], P('replica', 'tensor'), may hold values from -16 to 16
- span_kv: bfloat16 [8192, 4096], P('replica', 'tensor'), may hold values from -6 to 6, as said below
- kv_pool: bfloat16 [512, 128, 4096], P('replica', None, 'tensor'), may hold values from -8 to 8, as said below
- hit_owner: int32 [1024, 1], P('replica'), may hold values from 0 to 31; in each aligned block of 32 rows (0 to 31, 32 to 63, ...) at most 2 rows name the same one
- hit_slot: int32 [1024], P('replica'), may hold values from 0 to 15
- decode_query: bfloat16 [1024, 8192], P('replica', 'tensor'), may hold values from -16 to 16
- decode_kv: bfloat16 [1024, 4096], P('replica', 'tensor'), may hold values from -6 to 6, as said below
- decode_table: int32 [1024, 4], P('replica'), may hold values from 0 to 15
- decode_length: int32 [32, 32], P('replica'), may hold values from 1 to 512, 8192 in all within a row
Outputs:
- span_out: bfloat16 [8192, 8192], P('replica', 'tensor')
- decode_out: bfloat16 [1024, 8192], P('replica', 'tensor')
Inputs may be any that keep to these rules, and one draw needn't show every extreme that they name: `hit_owner`: among the 32 hits of one replica, at most 2 name the same owner. `kv_pool`: the 2 copies of a head are equal. `span_kv`: the 2 copies of a head are equal. `decode_kv`: the 2 copies of a head are equal.
All inputs are finite; a program needn't handle non-finite values.
Results may differ from a plain program's by a relative error of at most 0.009.
Values may be sent and summed in bfloat16 or wider, within the bound.
A program may use at most 64 MiB of HBM per device.

v0:
```python
import math

import jax
import jax.numpy as jnp
from jax import lax
from jax.sharding import PartitionSpec as P

HD = 128


def split_pairs(mine):
    return mine.reshape(mine.shape[:-1] + (mine.shape[-1] // (2 * HD), 2, HD))


def fold_block(carried, queries, key_rows, value_rows, allowed, inv_root):
    highest, weight_sum, mixture = carried
    scores = (
        jnp.einsum("rkgh,lkh->kgrl", queries, key_rows, preferred_element_type=jnp.float32)
        * inv_root
    )
    masked = jnp.where(allowed, scores, -1e30)
    raised = jnp.maximum(highest, jnp.max(masked, axis=-1))
    weights = jnp.where(allowed, jnp.exp(masked - raised[..., None]), 0.0)
    shrink = jnp.exp(highest - raised)
    weight_sum = weight_sum * shrink + jnp.sum(weights, axis=-1)
    mixture = mixture * shrink[..., None] + jnp.einsum(
        "kgrl,lkh->kgrh",
        weights.astype(jnp.bfloat16),
        value_rows,
        preferred_element_type=jnp.float32,
    )
    return (raised, weight_sum, mixture)


def local(
    span_query,
    span_kv,
    kv_pool,
    hit_owner,
    hit_slot,
    decode_query,
    decode_kv,
    decode_table,
    decode_length,
):
    replicas = lax.axis_size("replica")
    my_replica = lax.axis_index("replica")
    hit_total = hit_owner.shape[0]
    pool_slots, block_len, columns = kv_pool.shape
    capacity = max(2, 2 * hit_total // replicas)
    inv_root = HD ** (-0.5)
    all_owner, all_slot = (
        lax.all_gather(hit_owner[:, 0], "replica", axis=0, tiled=True),
        lax.all_gather(hit_slot, "replica", axis=0, tiled=True),
    )
    all_owner = all_owner.reshape(replicas, hit_total)
    all_slot = all_slot.reshape(replicas, hit_total)
    asked_here = all_owner == my_replica
    ranking = jnp.cumsum(asked_here.astype(jnp.int32), axis=1) - 1
    chosen = asked_here[:, None, :] & (
        ranking[:, None, :] == jnp.arange(capacity, dtype=jnp.int32)[None, :, None]
    )
    send_slot = jnp.sum(jnp.where(chosen, all_slot[:, None, :], 0), axis=2)
    arrived = lax.all_to_all(kv_pool[send_slot], "replica", split_axis=0, concat_axis=0, tiled=True)
    own_owner = hit_owner[:, 0]
    per_owner = jnp.sum(own_owner[None, :] == jnp.arange(replicas)[:, None], axis=1)
    fetched = arrived.reshape(replicas * capacity, block_len, columns)
    usable_blocks = (jnp.arange(capacity)[None, :] < per_owner[:, None]).reshape(
        replicas * capacity
    )
    prefix = split_pairs(fetched)
    fresh = split_pairs(span_kv)
    kv_local = fresh.shape[1]
    span_len = span_query.shape[0]
    group = span_query.shape[1] // (HD * kv_local)
    queries = span_query.reshape(span_len, kv_local, group, HD)
    causal = (jnp.arange(span_len)[:, None] >= jnp.arange(span_len)[None, :])[None, None]
    initial = (
        jnp.full((kv_local, group, span_len), -1e30, jnp.float32),
        jnp.zeros((kv_local, group, span_len), jnp.float32),
        jnp.zeros((kv_local, group, span_len, HD), jnp.float32),
    )
    carried = fold_block(initial, queries, fresh[:, :, 0], fresh[:, :, 1], causal, inv_root)
    block_count = prefix.shape[0]
    stride = math.gcd(block_count, 8)

    def prefix_step(counter, carried):
        first_block = counter * stride
        window = lax.dynamic_slice_in_dim(prefix, first_block, stride, 0).reshape(
            (stride * block_len,) + prefix.shape[2:]
        )
        usable = lax.dynamic_slice_in_dim(usable_blocks, first_block, stride, 0)
        allowed = jnp.repeat(usable, block_len)[None, None, None, :]
        return fold_block(carried, queries, window[:, :, 0], window[:, :, 1], allowed, inv_root)

    highest, weight_sum, mixture = lax.fori_loop(0, block_count // stride, prefix_step, carried)
    span_out = (
        jnp.transpose(mixture / weight_sum[..., None], (2, 0, 1, 3))
        .reshape(span_len, -1)
        .astype(jnp.bfloat16)
    )
    pool_pairs = split_pairs(kv_pool)
    own_pairs = split_pairs(decode_kv)
    dec_count, max_blocks = decode_table.shape
    dec_queries = decode_query.reshape(dec_count, kv_local, group, HD)
    pool_keys = pool_pairs[:, :, :, 0].reshape(pool_slots * block_len, kv_local, HD)
    pool_values = pool_pairs[:, :, :, 1].reshape(pool_slots * block_len, kv_local, HD)
    scores = (
        jnp.einsum("dkgh,lkh->dkgl", dec_queries, pool_keys, preferred_element_type=jnp.float32)
        * inv_root
    )
    scores = scores.reshape(dec_count, kv_local, group, pool_slots, block_len)
    picked = jnp.take_along_axis(scores, decode_table[:, None, None, :, None], axis=3)
    positions = jnp.arange(max_blocks)[:, None] * block_len + jnp.arange(block_len)[None, :]
    usable = positions[None, None, None] < decode_length[0][:, None, None, None, None]
    masked = jnp.where(usable, picked, -1e30)
    own_score = (
        jnp.einsum(
            "dkgh,dkh->dkg", dec_queries, own_pairs[:, :, 0], preferred_element_type=jnp.float32
        )
        * inv_root
    )
    peak = jnp.maximum(jnp.max(masked, axis=(3, 4)), own_score)
    weights = jnp.where(usable, jnp.exp(masked - peak[..., None, None]), 0.0)
    own_weight = jnp.exp(own_score - peak)
    dec_sum = jnp.sum(weights, axis=(3, 4)) + own_weight
    one_hot = (decode_table[:, :, None] == jnp.arange(pool_slots)[None, None, :]).astype(
        jnp.bfloat16
    )
    spread = jnp.einsum(
        "dkgbt,dbp->dkgpt",
        weights.astype(jnp.bfloat16),
        one_hot,
        preferred_element_type=jnp.float32,
    )
    spread = spread.astype(jnp.bfloat16).reshape(dec_count, kv_local, group, pool_slots * block_len)
    dec_mix = jnp.einsum("dkgl,lkh->dkgh", spread, pool_values, preferred_element_type=jnp.float32)
    own_rounded = lax.optimization_barrier(own_weight.astype(jnp.bfloat16)).astype(jnp.float32)
    dec_mix = (
        dec_mix + own_rounded[..., None] * own_pairs[:, :, 1].astype(jnp.float32)[:, :, None, :]
    )
    decode_out = (dec_mix / dec_sum[..., None]).reshape(dec_count, -1).astype(jnp.bfloat16)
    return (span_out, decode_out)


def solution(mesh):
    placed = (
        P("replica", "tensor"),
        P("replica", "tensor"),
        P("replica", None, "tensor"),
        P("replica", None),
        P("replica"),
        P("replica", "tensor"),
        P("replica", "tensor"),
        P("replica", None),
        P("replica", None),
    )
    return jax.shard_map(
        local,
        mesh=mesh,
        in_specs=placed,
        out_specs=(P("replica", "tensor"), P("replica", "tensor")),
        check_vma=False,
    )
```

profile of v0, /device:TPU:68, one launch (start us, length us, event | category | flops | bytes accessed | tf_op | source)
XLA Modules:
  0.0 191.5 jit_solution(1119389804199669230)
XLA Ops:
  0.6 1.3 dynamic-slice
  4.2 21.4 %all-reduce.2 = (s32[1024]{0:T(1024)S(1)}, s32[1024]{0:T(1024)S(1)}) all-reduce(s32[1024]{0:T(1024)S(1)} %dynamic-update-slice.1, s32[1024]{0:T(1024)S(1)} %bitcast_dynamic-update-slice_fusion), channel_id=1, replica_groups=mesh['replica'=32,'tensor'=16] {'replica'}, use_global_device_ids=true, to_apply=%add.1 | all-reduce | flops 2048 | bytes 16384
  26.3 4.0 %gather_fusion = bf16[64,128,256]{2,1,0:T(8,128)(2,1)} fusion(bf16[16,128,256]{2,1,0:T(8,128)(2,1)} %param.13, s32[1024]{0:T(1024)S(1)} %pad_clamp_fusion), kind=kCustom, calls=%fused_computation | custom fusion | bytes 8388864 | tf_op jit(solution)/shard_map/gather | solution.py:64
  30.3 6.4 %copy.82 = bf16[64,128,256]{1,2,0:T(8,128)(2,1)} copy(bf16[64,128,256]{2,1,0:T(8,128)(2,1)} %gather_fusion) | data formatting | bytes 8388608 | tf_op jit(solution)/shard_map/gather | solution.py:64
  36.7 5.7 %all-to-all-start = ((bf16[32,2,128,256]{2,3,1,0:T(8,128)(2,1)}), bf16[32,2,128,256]{2,3,1,0:T(8,128)(2,1)}, u32[]{:S(2)}, u32[]{:S(2)}) async-start(bf16[32,2,128,256]{2,3,1,0:T(8,128)(2,1)} %bitcast.257), calls=%async_computation | async-start | bytes 8388608 | tf_op jit(solution)/shard_map/all_to_all | solution.py:64
  43.4 1.5 fusion.52
  52.8 94.0 %all-to-all-done = bf16[32,2,128,256]{2,3,1,0:T(8,128)(2,1)} async-done(((bf16[32,2,128,256]{2,3,1,0:T(8,128)(2,1)}), bf16[32,2,128,256]{2,3,1,0:T(8,128)(2,1)}, u32[]{:S(2)}, u32[]{:S(2)}) %all-to-all-start) | async-done | bytes 4194336 | tf_op jit(solution)/shard_map/all_to_all | solution.py:64
  146.8 43.5 %while.17 = (s32[]{:T(128)}, f32[1,4,256]{2,1,0:T(4,128)S(1)}, f32[1,4,256]{2,1,0:T(4,128)S(1)}, f32[1,4,256,128]{3,2,1,0:T(8,128)S(1)}, pred[64]{0:T(512)(128)(...) while((s32[]{:T(128)}, f32[1,4,256]{2,1,0:T(4,128)S(1)}, ...), condition=%wide.region_8.9_spmd, body=%wide.region_5.8_spmd.sunk | while | flops 550767616 | bytes 16585915 | solution.py:96
  149.1 1.7 fusion.66
  150.8 1.4 fusion.65
  154.6 1.7 fusion.66
  156.2 1.4 fusion.65
  160.0 1.7 fusion.66
  161.7 1.4 fusion.65
  165.4 1.7 fusion.66
  167.1 1.4 fusion.65
  170.9 1.7 fusion.66
  172.6 1.4 fusion.65
  176.3 1.7 fusion.66
  178.0 1.4 fusion.65
  181.8 1.7 fusion.66
  183.5 1.4 fusion.65
  187.2 1.7 fusion.66
  188.9 1.4 fusion.65
  (144 shorter events, 30.4 us)
Async XLA Ops:
  36.7 5.7 %copy-start = (bf16[16,128,256]{2,1,0:T(8,128)(2,1)S(1)}, bf16[16,128,256]{2,1,0:T(8,128)(2,1)}, u32[]{:S(2)}) copy-start(bf16[16,128,256]{2,1,0:T(8,128)(2,1)} %param.13) | copy-start | bytes 3145732
  36.7 6.0 %copy-start.4 = (bf16[256,256]{1,0:T(8,128)(2,1)S(1)}, bf16[256,256]{1,0:T(8,128)(2,1)}, u32[]{:S(2)}) copy-start(bf16[256,256]{1,0:T(8,128)(2,1)} %param.12) | copy-start | bytes 393220
  36.7 6.1 %copy-start.1 = (bf16[256,512]{1,0:T(8,128)(2,1)S(1)}, bf16[256,512]{1,0:T(8,128)(2,1)}, u32[]{:S(2)}) copy-start(bf16[256,512]{1,0:T(8,128)(2,1)} %param.11) | copy-start | bytes 786436
  36.7 6.5 %copy-start.8 = (s32[32,1]{0,1:T(1,128)S(1)}, s32[32,1]{0,1:T(1,128)}, u32[]{:S(2)}) copy-start(s32[32,1]{0,1:T(1,128)} %param.14) | copy-start | bytes 388
  36.7 110.2 %all-to-all-start = ((bf16[32,2,128,256]{2,3,1,0:T(8,128)(2,1)}), bf16[32,2,128,256]{2,3,1,0:T(8,128)(2,1)}, u32[]{:S(2)}, u32[]{:S(2)}) async-start(bf16[32,2,128,256]{2,3,1,0:T(8,128)(2,1)} %bitcast.257), calls=%async_computation | async-start | bytes 8388608 | tf_op jit(solution)/shard_map/all_to_all | solution.py:64
  42.4 2.7 %copy-start.3 = (bf16[32,512]{1,0:T(8,128)(2,1)S(1)}, bf16[32,512]{1,0:T(8,128)(2,1)}, u32[]{:S(2)}) copy-start(bf16[32,512]{1,0:T(8,128)(2,1)} %param.16) | copy-start | bytes 98308
  44.9 1.3 copy-start.5
  45.0 2.7 %copy-start.6 = (bf16[32,256]{1,0:T(8,128)(2,1)S(1)}, bf16[32,256]{1,0:T(8,128)(2,1)}, u32[]{:S(2)}) copy-start(bf16[32,256]{1,0:T(8,128)(2,1)} %param.17) | copy-start | bytes 49156
  45.0 3.0 %copy-start.7 = (s32[1,32]{1,0:T(1,128)S(1)}, s32[1,32]{1,0:T(1,128)}, u32[]{:S(2)}) copy-start(s32[1,32]{1,0:T(1,128)} %param.19) | copy-start | bytes 388
  46.3 5.5 %copy-start.2 = (bf16[256,512]{1,0:T(8,128)(2,1)S(1)}, bf16[256,512]{1,0:T(8,128)(2,1)}, u32[]{:S(2)}) copy-start(bf16[256,512]{1,0:T(8,128)(2,1)} %param.11) | copy-start | bytes 786436
where the time goes:
time: 192 us
  waiting for transfers between devices  94 us (49%)
  local copies, waits for them, and re-layouts  32.2 us (17%)
  matrix products  21.7 us (11%)
  blocking collectives  21.4 us (11%)
  other arithmetic  14.3 us (7%)
  starting transfers between devices  5.67 us (3%)
    all_to_all x1, waiting for transfers between devices, local(): lax.all_to_all(kv_pool[send_slot], 'replica', split_axis=0, concat_axis=0...  94 us
    unnamed x1, blocking collectives  21.4 us
    dot_general x9, matrix products, fold_block(): jnp.einsum('kgrl,lkh->kgrh', weights.astype(jnp.bfloat16), value_rows, pr...  13.8 us
    reduce_sum x9, other arithmetic, fold_block(): weight_sum = weight_sum * shrink + jnp.sum(weights, axis=-1)  11.6 us
    dynamic_slice x16, local copies, waits for them, and re-layouts, prefix_step(): lax.dynamic_slice_in_dim(prefix, first_block, stride, 0)  10.9 us
    gather x2, local copies, waits for them, and re-layouts, local(): kv_pool[send_slot]  10.3 us
    dot_general x9, matrix products, fold_block(): jnp.einsum('rkgh,lkh->kgrl', queries, key_rows, preferred_element_type=jn...  6.3 us
    all_to_all x1, starting transfers between devices, local(): lax.all_to_all(kv_pool[send_slot], 'replica', split_axis=0, concat_axis=0...  5.67 us
  transfers between devices with their start and end apart: 1, of which 1 were waited for; matrix products, arithmetic and copies ran while one was open for 5% of the time, Pallas kernels for 0%

commit v1 on v0

v1 whole, which is shorter than its diff:
```python
import functools
import math

import jax
import jax.numpy as jnp
from jax import lax
from jax.experimental import pallas as pl
from jax.experimental.pallas import tpu as pltpu
from jax.sharding import PartitionSpec as P

MESH = pl.DeviceIdType.MESH
HD = 128
NZ = 8
HALF = 64
CHUNKS = 4
SCALE = HD ** (-0.5) * math.log2(math.e)
LOW = -1e30


def nt_dot(a, b):
    return lax.dot_general(a, b, (((1,), (1,)), ((), ())), preferred_element_type=jnp.float32)


def column(row):
    n = row.shape[1]
    eye = lax.broadcasted_iota(jnp.int32, (n, n), 0) == lax.broadcasted_iota(jnp.int32, (n, n), 1)
    return jnp.sum(jnp.where(eye, jnp.broadcast_to(row, (n, n)), 0.0), axis=1, keepdims=True)


def as_row(replicated):
    eye = lax.broadcasted_iota(jnp.int32, (128, 128), 0) == lax.broadcasted_iota(
        jnp.int32, (128, 128), 1
    )
    return jnp.sum(jnp.where(eye, replicated, 0.0), axis=0, keepdims=True)


def kernel(
    owner_s,
    slot_s,
    table_ref,
    length_ref,
    dq_ref,
    dkv_ref,
    skv_ref,
    q_hbm,
    pool_hbm,
    span_out,
    decode_out,
    pool_v,
    qall,
    up1,
    up2,
    up3,
    down1,
    down2,
    down3,
    far,
    stage,
    inbox,
    tabs,
    tabs_s,
    acc,
    top,
    total,
    part_out,
    part_in,
    stat_out,
    stat_in,
    load_sem,
    zsend,
    zrecv,
    psend,
    precv,
    tsend,
    trecv,
    smem_sem,
    qsend,
    qrecv,
    osend,
    orecv,
    ssend,
    srecv,
):
    r = lax.axis_index("replica")
    t = lax.axis_index("tensor")
    yl, z, c = r // 16, (r // 2) % NZ, r % 2
    xh = t % 2
    tx = t + 1 - 2 * xh

    def at_z(step):
        return (yl * 16 + ((z + step + NZ) % NZ) * 2 + c, t)

    def peer(e):
        py = yl if e < 2 else 1 - yl
        pc = c if e % 2 == 0 else 1 - c
        return (py, pc)

    def peer_id(e):
        py, pc = peer(e)
        return (py * 16 + z * 2 + pc, t)

    xid = (r, tx)
    buf = ((up1, up2, up3, far), (down1, down2, down3, far))
    ahead = (at_z(1), at_z(-1))

    barrier = pltpu.get_barrier_semaphore()
    for other in ahead + (peer_id(1), peer_id(2), peer_id(3), xid):
        pl.semaphore_signal(barrier, inc=1, device_id=other, device_id_type=MESH)

    loads = [pltpu.make_async_copy(pool_hbm, pool_v, load_sem.at[0])]
    for h in range(4):
        loads.append(
            pltpu.make_async_copy(
                q_hbm.at[:, pl.ds(h * HD, HD)], qall.at[h], load_sem.at[1 + h]
            )
        )
    for copy in loads:
        copy.start()

    pl.semaphore_wait(barrier, 6)

    per = 16 // CHUNKS

    def ring(d, k, ch):
        rows = pl.ds(ch * per, per)
        if k == 1:
            src = pool_hbm.at[rows, pl.ds(pl.multiple_of(xh * HALF, HALF), HALF), :]
        else:
            src = buf[d][k - 2].at[rows]
        return pltpu.make_async_remote_copy(
            src_ref=src,
            dst_ref=buf[d][k - 1].at[rows],
            send_sem=zsend.at[d, k - 1, ch],
            recv_sem=zrecv.at[d, k - 1, ch],
            device_id=ahead[d],
            device_id_type=MESH,
        )

    def chunks_of(d, k):
        if k < 4:
            return range(CHUNKS)
        return range(CHUNKS // 2) if d == 0 else range(CHUNKS // 2, CHUNKS)

    for ch in range(CHUNKS):
        for d in range(2):
            ring(d, 1, ch).start()

    def query_copy(h):
        return pltpu.make_async_remote_copy(
            src_ref=q_hbm.at[:, pl.ds(h * HD, HD)],
            dst_ref=qall.at[4 + h],
            send_sem=qsend.at[h],
            recv_sem=qrecv.at[h],
            device_id=xid,
            device_id_type=MESH,
        )

    for h in range(4):
        query_copy(h).start()

    lane = lax.broadcasted_iota(jnp.int32, (8, 128), 1)
    lane_owner, lane_rank = lane // 2, lane % 2

    def note_hit(i, carried):
        table, seen = carried
        match = lane_owner == owner_s[i]
        table = jnp.where(match & (seen == lane_rank), slot_s[i], table)
        return table, seen + match.astype(jnp.int32)

    table, _ = lax.fori_loop(
        0,
        32,
        note_hit,
        (jnp.full((8, 128), -1, jnp.int32), jnp.zeros((8, 128), jnp.int32)),
    )
    tabs[0] = table

    def table_copy(e):
        return pltpu.make_async_remote_copy(
            src_ref=tabs.at[0],
            dst_ref=tabs.at[e],
            send_sem=tsend.at[e],
            recv_sem=trecv.at[e],
            device_id=peer_id(e),
            device_id_type=MESH,
        )

    for e in range(1, 4):
        table_copy(e).start()

    loads[0].wait()
    for e in range(4):
        if e:
            table_copy(e).wait_recv()
        moved = pltpu.make_async_copy(tabs.at[e], tabs_s.at[e], smem_sem.at[e])
        moved.start()
        moved.wait()

    def plane_z(p):
        step = -p if p < 5 else p - 4
        return (z + step + NZ) % NZ

    def hand_copy(p, e):
        return pltpu.make_async_remote_copy(
            src_ref=stage.at[p, e],
            dst_ref=inbox.at[p, e],
            send_sem=psend.at[p, e],
            recv_sem=precv.at[p, e],
            device_id=peer_id(e),
            device_id_type=MESH,
        )

    def hand_out(p):
        owner = yl * 16 + plane_z(p) * 2 + c
        for e in (3, 2, 1, 0):
            for rank in range(2):
                slot = jnp.clip(tabs_s[e, 0, owner * 2 + rank], 0, 15)
                if p == 0:
                    rows = pool_v[slot, pl.ds(pl.multiple_of(xh * HALF, HALF), HALF), :]
                elif p < 5:
                    rows = buf[0][p - 1][slot]
                else:
                    rows = buf[1][p - 5][slot]
                place = pl.ds(rank * HALF, HALF)
                if e == 0:
                    inbox[p, 0, place, :] = rows
                else:
                    stage[p, e, place, :] = rows
            if e:
                hand_copy(p, e).start()

    hand_out(0)

    count = 32
    dq = jnp.concatenate([dq_ref[:, pl.ds(g * HD, HD)] for g in range(4)], axis=0)
    lengths = column(length_ref[...].astype(jnp.float32))
    names = [column(table_ref[b : b + 1, :].astype(jnp.float32)) for b in range(4)]
    spot = lax.broadcasted_iota(jnp.int32, (count, HD), 1).astype(jnp.float32)

    def times(block):
        name = jnp.float32(1) * block
        seen = jnp.zeros((count, HD), jnp.float32)
        for b in range(4):
            limit = jnp.where(names[b] == name, lengths - 128.0 * b, 0.0)
            seen = seen + jnp.where(spot < limit, 1.0, 0.0)
        return jnp.concatenate([seen] * 4, axis=0)

    own_key = jnp.concatenate([dkv_ref[:, :HD].astype(jnp.float32)] * 4, axis=0)
    own_value = jnp.concatenate([dkv_ref[:, HD:].astype(jnp.float32)] * 4, axis=0)
    own_score = jnp.sum(dq.astype(jnp.float32) * own_key, axis=1, keepdims=True)

    def decode_step(it, carried):
        highest, weight_sum, mixture = carried
        rows = pool_v[pl.ds(it * 4, 4)].reshape(4 * HD, 2 * HD)
        scores = nt_dot(dq, rows[:, :HD])
        seen = jnp.concatenate([times((it * 4 + i).astype(jnp.float32)) for i in range(4)], axis=1)
        masked = jnp.where(seen > 0.0, scores, LOW)
        raised = jnp.maximum(highest, jnp.max(masked, axis=1, keepdims=True))
        weights = jnp.exp2((masked - raised) * SCALE)
        shrink = jnp.exp2((highest - raised) * SCALE)
        weight_sum = weight_sum * shrink + jnp.sum(weights * seen, axis=1, keepdims=True)
        spread = (weights.astype(jnp.bfloat16).astype(jnp.float32) * seen).astype(jnp.bfloat16)
        mixture = mixture * shrink + jnp.dot(
            spread, rows[:, HD:], preferred_element_type=jnp.float32
        )
        return raised, weight_sum, mixture

    _, weight_sum, mixture = lax.fori_loop(
        0, 4, decode_step, (own_score, jnp.ones((128, 1), jnp.float32), own_value)
    )
    mixed = (mixture / weight_sum).astype(jnp.bfloat16)
    for g in range(4):
        decode_out[:, pl.ds(g * HD, HD)] = mixed[g * count : (g + 1) * count]

    for copy in loads[1:]:
        copy.wait()
    fresh_keys, fresh_values = skv_ref[:, :HD], skv_ref[:, HD:]
    causal = lax.broadcasted_iota(jnp.int32, (256, 256), 0) >= lax.broadcasted_iota(
        jnp.int32, (256, 256), 1
    )

    def fresh_step(h, carried):
        masked = jnp.where(causal, nt_dot(qall[h], fresh_keys), LOW)
        highest = jnp.max(masked, axis=1, keepdims=True)
        weights = jnp.exp2((masked - highest) * SCALE)
        top[h] = jnp.broadcast_to(highest, (256, HD))
        total[h] = weights[:, :HD] + weights[:, HD:]
        acc[h] = jnp.dot(
            weights.astype(jnp.bfloat16), fresh_values, preferred_element_type=jnp.float32
        )
        top[4 + h] = jnp.full((256, HD), LOW, jnp.float32)
        total[4 + h] = jnp.zeros((256, HD), jnp.float32)
        acc[4 + h] = jnp.zeros((256, HD), jnp.float32)
        return carried

    lax.fori_loop(0, 4, fresh_step, 0)
    for h in range(4):
        query_copy(h).wait_recv()

    cell = lax.broadcasted_iota(jnp.int32, (1, 512), 1) // HALF

    def attend(p, first, count):
        bias = jnp.zeros((1, 512), jnp.float32)
        for e in range(4):
            py, pc = peer(e)
            owner = py * 16 + plane_z(p) * 2 + pc
            for rank in range(2):
                asked = tabs_s[0, 0, owner * 2 + rank]
                bias = jnp.where(
                    (cell == 2 * e + rank) & (jnp.full((1, 512), asked, jnp.int32) < 0), LOW, bias
                )

        def fold(h, carried):
            rows = inbox[p].reshape(512, 2 * HD)
            scores = nt_dot(qall[h], rows[:, :HD]) + bias
            highest = top[h][:, :1]
            raised = jnp.maximum(highest, jnp.max(scores, axis=1, keepdims=True))
            weights = jnp.exp2((scores - raised) * SCALE)
            shrink = jnp.exp2((highest - raised) * SCALE)
            top[h] = jnp.broadcast_to(raised, (256, HD))
            total[h] = total[h] * shrink + (
                (weights[:, :HD] + weights[:, HD : 2 * HD])
                + (weights[:, 2 * HD : 3 * HD] + weights[:, 3 * HD :])
            )
            acc[h] = acc[h] * shrink + jnp.dot(
                weights.astype(jnp.bfloat16), rows[:, HD:], preferred_element_type=jnp.float32
            )
            return carried

        lax.fori_loop(first, first + count, fold, 0)

    def collect(p):
        for e in range(1, 4):
            hand_copy(p, e).wait_recv()

    planes = ((0,), (1, 5), (2, 6), (3, 7), (4,))
    for k in range(1, 5):
        for i in range(CHUNKS):
            for d in range(2):
                if i < len(chunks_of(d, k)):
                    ch = chunks_of(d, k)[i]
                    ring(d, k, ch).wait_recv()
                    if k < 4 and ch in chunks_of(d, k + 1):
                        ring(d, k + 1, ch).start()
        for p in planes[k]:
            hand_out(p)
        for p in planes[k - 1]:
            collect(p)
            attend(p, 0, 8)

    def part_copy(h):
        return pltpu.make_async_remote_copy(
            src_ref=part_out.at[h],
            dst_ref=part_in.at[h],
            send_sem=osend.at[h],
            recv_sem=orecv.at[h],
            device_id=xid,
            device_id_type=MESH,
        )

    def stat_copy(h):
        return pltpu.make_async_remote_copy(
            src_ref=stat_out.at[h],
            dst_ref=stat_in.at[h],
            send_sem=ssend.at[h],
            recv_sem=srecv.at[h],
            device_id=xid,
            device_id_type=MESH,
        )

    collect(4)
    attend(4, 4, 4)
    for h in range(4):
        part_out[h] = acc[4 + h].astype(jnp.bfloat16)
        stat_out[h] = jnp.zeros((8, HD), jnp.float32)
        for i in range(2):
            rows = pl.ds(i * HD, HD)
            sums = jnp.sum(total[4 + h, rows, :], axis=1, keepdims=True)
            stat_out[h, i : i + 1, :] = as_row(top[4 + h, rows, :])
            stat_out[h, 2 + i : 3 + i, :] = as_row(jnp.broadcast_to(sums, (HD, HD)))
        part_copy(h).start()
        stat_copy(h).start()
    attend(4, 0, 4)
    for h in range(4):
        part_copy(h).wait_recv()
        stat_copy(h).wait_recv()
        for i in range(2):
            rows = pl.ds(i * HD, HD)
            here, there = top[h, rows, :][:, :1], column(stat_in[h, i : i + 1, :])
            peak = jnp.maximum(here, there)
            keep, take = jnp.exp2((here - peak) * SCALE), jnp.exp2((there - peak) * SCALE)
            sums = (
                jnp.sum(total[h, rows, :], axis=1, keepdims=True) * keep
                + column(stat_in[h, 2 + i : 3 + i, :]) * take
            )
            mixed = acc[h, rows, :] * keep + part_in[h, rows, :].astype(jnp.float32) * take
            span_out[rows, pl.ds(h * HD, HD)] = (mixed / sums).astype(jnp.bfloat16)

    for k in range(1, 5):
        for d in range(2):
            for ch in chunks_of(d, k):
                ring(d, k, ch).wait_send()
    for h in range(4):
        query_copy(h).wait_send()
        part_copy(h).wait_send()
        stat_copy(h).wait_send()
    for e in range(1, 4):
        table_copy(e).wait_send()
        for p in range(NZ):
            hand_copy(p, e).wait_send()


def local(
    span_query,
    span_kv,
    kv_pool,
    hit_owner,
    hit_slot,
    decode_query,
    decode_kv,
    decode_table,
    decode_length,
):
    vmem = pl.BlockSpec(memory_space=pltpu.VMEM)
    smem = pl.BlockSpec(memory_space=pltpu.SMEM)
    hbm = pl.BlockSpec(memory_space=pl.ANY)
    dma = pltpu.SemaphoreType.DMA
    bf16, f32 = jnp.bfloat16, jnp.float32
    return pl.pallas_call(
        kernel,
        out_shape=(
            jax.ShapeDtypeStruct(span_query.shape, bf16),
            jax.ShapeDtypeStruct(decode_query.shape, bf16),
        ),
        in_specs=[smem, smem, vmem, vmem, vmem, vmem, vmem, hbm, hbm],
        out_specs=(vmem, vmem),
        scratch_shapes=[
            pltpu.VMEM((16, 128, 256), bf16),
            pltpu.VMEM((8, 256, HD), bf16),
        ]
        + [pltpu.VMEM((16, HALF, 256), bf16)] * 7
        + [
            pltpu.VMEM((NZ, 4, 2 * HALF, 256), bf16),
            pltpu.VMEM((NZ, 4, 2 * HALF, 256), bf16),
            pltpu.VMEM((4, 8, 128), jnp.int32),
            pltpu.SMEM((4, 8, 128), jnp.int32),
            pltpu.VMEM((8, 256, HD), f32),
            pltpu.VMEM((8, 256, HD), f32),
            pltpu.VMEM((8, 256, HD), f32),
            pltpu.VMEM((4, 256, HD), bf16),
            pltpu.VMEM((4, 256, HD), bf16),
            pltpu.VMEM((4, 8, 128), f32),
            pltpu.VMEM((4, 8, 128), f32),
            dma((5,)),
            dma((2, 4, CHUNKS)),
            dma((2, 4, CHUNKS)),
            dma((NZ, 4)),
            dma((NZ, 4)),
            dma((4,)),
            dma((4,)),
            dma((4,)),
            dma((4,)),
            dma((4,)),
            dma((4,)),
            dma((4,)),
            dma((4,)),
            dma((4,)),
        ],
        compiler_params=pltpu.CompilerParams(
            collective_id=0, has_side_effects=True, vmem_limit_bytes=56 * 1024 * 1024
        ),
        cost_estimate=pl.CostEstimate(
            flops=5 * 10**9, bytes_accessed=3 * 2**20, transcendentals=10**7
        ),
        name="spanned_attention",
    )(
        hit_owner.reshape(-1),
        hit_slot,
        decode_table.T,
        decode_length,
        decode_query,
        decode_kv,
        span_kv,
        span_query,
        kv_pool,
    )


def solution(mesh):
    placed = (
        P("replica", "tensor"),
        P("replica", "tensor"),
        P("replica", None, "tensor"),
        P("replica", None),
        P("replica"),
        P("replica", "tensor"),
        P("replica", "tensor"),
        P("replica", None),
        P("replica", None),
    )
    return jax.shard_map(
        local,
        mesh=mesh,
        in_specs=placed,
        out_specs=(P("replica", "tensor"), P("replica", "tensor")),
        check_vma=False,
    )
```

time: 192 us -> 82.2 us (0.43)
  the two profiles are of different devices: /device:TPU:68 before, /device:TPU:16 now
where the time goes in v1:
time: 82.2 us; the launch traced here: 82 us
  Pallas kernels  79.1 us (96%)
  local copies, waits for them, and re-layouts  2.29 us (3%)
    pallas_call x1, Pallas kernels, local(): pl.pallas_call(kernel, out_shape=(jax.ShapeDtypeStruct(span_query.shape,...  79.1 us
    unnamed x4, local copies, waits for them, and re-layouts  2.29 us

profile of v1, /device:TPU:16, one launch (start us, length us, event | category | flops | bytes accessed | tf_op | source)
XLA Modules:
  0.0 82.0 jit_solution(7470735012948579453)
XLA Ops:
  0.6 79.1 %spanned_attention.1 = (bf16[256,512]{1,0:T(8,128)(2,1)}, bf16[32,512]{1,0:T(8,128)(2,1)}) custom-call(s32[32]{0:T(128)} %bitcast.3, s32[32]{0:T(128)} %slot_s.1, s32[4,32]{1,0:T(4,128)} %bitcast.2, s32[1,32]{1,0:T(1,128)} %length_ref.1, bf16[32,512]{1,0:T(8,128)(2,1)} %dq_ref.1, bf16[32,256]{1,0:T(8,128)(2,1)} %dkv_ref.1, bf16[256,256]{1,0:T(8,128)(2,1)} %skv_ref.1, ...), custom_call_target="tpu_custom_call" | custom-call | flops 5000000000 | bytes 3145728 | tf_op jit(solution)/shard_map/spanned_attention/pallas_call | solution.py:429
  79.7 0.0 copy-start
  79.7 1.7 %copy.13 = bf16[256,512]{1,0:T(8,128)(2,1)} copy(bf16[256,512]{1,0:T(8,128)(2,1)} %get-tuple-element.4) | data formatting | bytes 524288
  81.4 0.0 copy-done
  81.4 0.6 copy.14
Async XLA Ops:
  79.7 1.7 %copy-start = (bf16[32,512]{1,0:T(8,128)(2,1)S(1)}, bf16[32,512]{1,0:T(8,128)(2,1)}, u32[]{:S(2)}) copy-start(bf16[32,512]{1,0:T(8,128)(2,1)} %get-tuple-element.5) | copy-start | bytes 98308

commit v2 on v1

v2 whole, which is shorter than its diff:
```python
import functools
import math

import jax
import jax.numpy as jnp
from jax import lax
from jax.experimental import pallas as pl
from jax.experimental.pallas import tpu as pltpu
from jax.sharding import PartitionSpec as P

MESH = pl.DeviceIdType.MESH
HD = 128
NZ = 8
HALF = 64
CHUNKS = 2
PIECE = HALF // CHUNKS
TILE = 512
SCALE = HD ** (-0.5) * math.log2(math.e)
LOW = -1e30


def nt_dot(a, b):
    return lax.dot_general(a, b, (((1,), (1,)), ((), ())), preferred_element_type=jnp.float32)


def column(row):
    n = row.shape[1]
    eye = lax.broadcasted_iota(jnp.int32, (n, n), 0) == lax.broadcasted_iota(jnp.int32, (n, n), 1)
    return jnp.sum(jnp.where(eye, jnp.broadcast_to(row, (n, n)), 0.0), axis=1, keepdims=True)


def as_row(replicated):
    eye = lax.broadcasted_iota(jnp.int32, (128, 128), 0) == lax.broadcasted_iota(
        jnp.int32, (128, 128), 1
    )
    return jnp.sum(jnp.where(eye, replicated, 0.0), axis=0, keepdims=True)


def kernel(
    owner_s,
    slot_s,
    table_ref,
    length_ref,
    dq_ref,
    dkv_ref,
    skv_ref,
    q_hbm,
    pool_hbm,
    span_out,
    decode_out,
    pool_v,
    qall,
    hop_bufs,
    stage,
    near_stage,
    far_stage,
    far_in,
    inbox,
    tabs,
    tabs_s,
    bundle,
    near,
    near_s,
    keys,
    values,
    scored,
    acc,
    top,
    part_out,
    part_in,
    stat_out,
    stat_in,
    load_sem,
    zsend,
    zrecv,
    psend,
    precv,
    nsend,
    nrecv,
    fsend,
    frecv,
    gsend,
    grecv,
    tsend,
    trecv,
    bsend,
    brecv,
    smem_sem,
    qsend,
    qrecv,
    osend,
    orecv,
    ssend,
    srecv,
):
    r = lax.axis_index("replica")
    t = lax.axis_index("tensor")
    yl, z, c = r // 16, (r // 2) % NZ, r % 2
    xh = t % 2
    tx = t + 1 - 2 * xh

    def plane(step):
        return (z + step + NZ) % NZ

    def peer(e):
        return (yl if e < 2 else 1 - yl), (c if e % 2 == 0 else 1 - c)

    def device(e, step):
        py, pc = peer(e)
        return (py * 16 + plane(step) * 2 + pc, t)

    xid = (r, tx)
    up_down = (1, -1)
    partners = [device(e, 0) for e in range(1, 4)] + [xid]
    partners += [device(e, step) for e in range(4) for step in (1, -1)]
    partners += [device(0, 2), device(0, -2)]

    barrier = pltpu.get_barrier_semaphore()
    for other in partners:
        pl.semaphore_signal(barrier, inc=1, device_id=other, device_id_type=MESH)

    loads = [pltpu.make_async_copy(pool_hbm, pool_v, load_sem.at[0])]
    for h in range(4):
        loads.append(
            pltpu.make_async_copy(
                q_hbm.at[:, pl.ds(h * HD, HD)], qall.at[pl.ds(h * 256, 256)], load_sem.at[1 + h]
            )
        )
    for copy in loads:
        copy.start()

    def remote(src, dst, send, recv, where):
        return pltpu.make_async_remote_copy(
            src_ref=src,
            dst_ref=dst,
            send_sem=send,
            recv_sem=recv,
            device_id=where,
            device_id_type=MESH,
        )

    def ring(d, k, ch):
        if k == 1:
            first = pl.multiple_of(xh * HALF + ch * PIECE, PIECE)
            src = pool_hbm.at[:, pl.ds(first, PIECE), :]
        else:
            src = hop_bufs[d][0][ch]
        return remote(
            src,
            hop_bufs[d][k - 1][ch],
            zsend.at[d, k - 1, ch],
            zrecv.at[d, k - 1, ch],
            device(0, up_down[d]),
        )

    both = [(d, ch) for ch in range(CHUNKS) for d in range(2)]

    pl.semaphore_wait(barrier, len(partners))
    for d, ch in both:
        ring(d, 1, ch).start()

    def query_copy(h):
        return remote(
            q_hbm.at[:, pl.ds(h * HD, HD)],
            qall.at[pl.ds((4 + h) * 256, 256)],
            qsend.at[h],
            qrecv.at[h],
            xid,
        )

    lane = lax.broadcasted_iota(jnp.int32, (8, 128), 1)
    lane_owner, lane_rank = lane // 2, lane % 2

    def note_hit(i, carried):
        table, seen = carried
        match = lane_owner == owner_s[i]
        table = jnp.where(match & (seen == lane_rank), slot_s[i], table)
        return table, seen + match.astype(jnp.int32)

    table, _ = lax.fori_loop(
        0,
        32,
        note_hit,
        (jnp.full((8, 128), -1, jnp.int32), jnp.zeros((8, 128), jnp.int32)),
    )
    tabs[0] = table

    def table_copy(e):
        return remote(tabs.at[0], tabs.at[e], tsend.at[e], trecv.at[e], device(e, 0))

    for e in range(1, 4):
        table_copy(e).start()
    for h in range(4):
        query_copy(h).start()

    steps = (1, 2, -1, -2)

    def bundle_copy(i):
        back = steps.index(-steps[i])
        return remote(bundle, near.at[back], bsend.at[back], brecv.at[back], device(0, steps[i]))

    def bundle_wait(i):
        return remote(bundle, near.at[i], bsend.at[i], brecv.at[i], device(0, steps[i]))

    bundle[...] = jnp.full((8, 128), -1, jnp.int32)
    for e in range(4):
        if e:
            table_copy(e).wait_recv()
        bundle[e : e + 1, :] = tabs[e, 0:1, :]
    for i in range(4):
        bundle_copy(i).start()
    moved = pltpu.make_async_copy(bundle, tabs_s, smem_sem.at[0])
    moved.start()
    loads[0].wait()
    moved.wait()

    def plane_of(p):
        return plane(-p if p < 5 else p - 4)

    def hand_copy(p, ch, e):
        return remote(
            stage.at[p if p < 3 else p - 2, ch, e],
            inbox.at[p, ch, e],
            psend.at[p, ch, e],
            precv.at[p, ch, e],
            device(e, 0),
        )

    def asked(rows_s, e, owner, rank):
        return jnp.clip(rows_s[e, owner * 2 + rank], 0, 15)

    def hand_out(p, ch):
        owner = yl * 16 + plane_of(p) * 2 + c
        for e in (3, 2, 1, 0):
            for rank in range(2):
                slot = asked(tabs_s, e, owner, rank)
                if p == 0:
                    first = pl.multiple_of(xh * HALF + ch * PIECE, PIECE)
                    rows = pool_v[slot, pl.ds(first, PIECE), :]
                else:
                    d, k = (0, p) if p < 5 else (1, p - 4)
                    rows = hop_bufs[d][k - 1][ch][slot]
                place = pl.ds(rank * PIECE, PIECE)
                if e == 0:
                    inbox[p, ch, 0, place, :] = rows
                else:
                    stage[p if p < 3 else p - 2, ch, e, place, :] = rows
            if e:
                hand_copy(p, ch, e).start()

    for ch in range(CHUNKS):
        hand_out(0, ch)

    count = 32
    dq = jnp.concatenate([dq_ref[:, pl.ds(g * HD, HD)] for g in range(4)], axis=0)
    lengths = column(length_ref[...].astype(jnp.float32))
    names = [column(table_ref[b : b + 1, :].astype(jnp.float32)) for b in range(4)]
    spot = lax.broadcasted_iota(jnp.int32, (count, HD), 1).astype(jnp.float32)

    def times(block):
        seen = jnp.zeros((count, HD), jnp.float32)
        for b in range(4):
            limit = jnp.where(names[b] == block, lengths - 128.0 * b, 0.0)
            seen = seen + jnp.where(spot < limit, 1.0, 0.0)
        return jnp.concatenate([seen] * 4, axis=0)

    own_key = jnp.concatenate([dkv_ref[:, :HD].astype(jnp.float32)] * 4, axis=0)
    own_value = jnp.concatenate([dkv_ref[:, HD:].astype(jnp.float32)] * 4, axis=0)
    own_score = jnp.sum(dq.astype(jnp.float32) * own_key, axis=1, keepdims=True)

    def decode_step(it, carried):
        highest, weight_sum, mixture = carried
        rows = pool_v[pl.ds(it * 4, 4)].reshape(4 * HD, 2 * HD)
        scores = nt_dot(dq, rows[:, :HD])
        seen = jnp.concatenate([times((it * 4 + i).astype(jnp.float32)) for i in range(4)], axis=1)
        masked = jnp.where(seen > 0.0, scores, LOW)
        raised = jnp.maximum(highest, jnp.max(masked, axis=1, keepdims=True))
        weights = jnp.exp2((masked - raised) * SCALE)
        shrink = jnp.exp2((highest - raised) * SCALE)
        weight_sum = weight_sum * shrink + jnp.sum(weights * seen, axis=1, keepdims=True)
        spread = (weights.astype(jnp.bfloat16).astype(jnp.float32) * seen).astype(jnp.bfloat16)
        mixture = mixture * shrink + jnp.dot(
            spread, rows[:, HD:], preferred_element_type=jnp.float32
        )
        return raised, weight_sum, mixture

    _, weight_sum, mixture = lax.fori_loop(
        0, 4, decode_step, (own_score, jnp.ones((128, 1), jnp.float32), own_value)
    )
    mixed = (mixture / weight_sum).astype(jnp.bfloat16)
    for g in range(4):
        decode_out[:, pl.ds(g * HD, HD)] = mixed[g * count : (g + 1) * count]

    def forward(ch):
        for d in range(2):
            ring(d, 1, ch).wait_recv()
            ring(d, 2, ch).start()

    forward(0)

    for copy in loads[1:]:
        copy.wait()
    fresh_keys = skv_ref[:, :HD]
    fresh_values = jnp.concatenate([skv_ref[:, HD:], jnp.ones((256, HD), jnp.bfloat16)], axis=1)
    causal = lax.broadcasted_iota(jnp.int32, (256, 256), 0) >= lax.broadcasted_iota(
        jnp.int32, (256, 256), 1
    )

    def fresh_step(h, carried):
        for i in range(2):
            rows = pl.ds(pl.multiple_of((2 * h + i) * 256, 256), 256)
            masked = jnp.where(causal, nt_dot(qall[rows, :], fresh_keys), LOW)
            highest = jnp.broadcast_to(jnp.max(masked, axis=1, keepdims=True), (256, HD))
            weights = jnp.concatenate(
                [
                    jnp.exp2((masked[:, j * HD : (j + 1) * HD] - highest) * SCALE)
                    for j in range(2)
                ],
                axis=1,
            )
            top[rows, :] = highest
            acc[rows, :] = jnp.dot(
                weights.astype(jnp.bfloat16), fresh_values, preferred_element_type=jnp.float32
            )
            rows = pl.ds(pl.multiple_of((4 + 2 * h + i) * 256, 256), 256)
            top[rows, :] = jnp.full((256, HD), LOW, jnp.float32)
            acc[rows, :] = jnp.zeros((256, 2 * HD), jnp.float32)
        return carried

    lax.fori_loop(0, 2, fresh_step, 0)
    forward(1)

    seen_key = jnp.broadcast_to(skv_ref[0:1, :HD].astype(jnp.float32), (PIECE, HD)).astype(
        jnp.bfloat16
    )

    def prepare(p, place):
        for ch in range(CHUNKS):
            for e in range(4):
                py, pc = peer(e)
                owner = py * 16 + plane_of(p) * 2 + pc
                for rank in range(2):
                    used = tabs_s[0, owner * 2 + rank] >= 0
                    cell = inbox[p, ch, e, pl.ds(rank * PIECE, PIECE), :]
                    rows = pl.ds(((ch * 4 + e) * 2 + rank) * PIECE, PIECE)
                    keys[place, rows, :] = jnp.where(used, cell[:, :HD], seen_key)
                    values[place, rows, :HD] = jnp.where(
                        used, cell[:, HD:], jnp.zeros((PIECE, HD), jnp.bfloat16)
                    )
                    values[place, rows, HD:] = jnp.where(
                        used,
                        jnp.ones((PIECE, HD), jnp.bfloat16),
                        jnp.zeros((PIECE, HD), jnp.bfloat16),
                    )

    def tile_rows(tile):
        if isinstance(tile, int):
            return pl.ds(tile * TILE, TILE)
        return pl.ds(pl.multiple_of(tile * TILE, TILE), TILE)

    def score(place, tile, slot):
        scored[slot] = nt_dot(qall[tile_rows(tile), :], keys[place])

    def fold(place, tile, slot):
        rows = tile_rows(tile)
        parts = [scored[slot, :, j * HD : (j + 1) * HD] for j in range(4)]
        highest = top[rows, :]
        most = jnp.maximum(jnp.maximum(parts[0], parts[1]), jnp.maximum(parts[2], parts[3]))
        raised = jnp.maximum(
            highest, jnp.broadcast_to(jnp.max(most, axis=1, keepdims=True), (TILE, HD))
        )
        weights = jnp.concatenate(
            [jnp.exp2((part - raised) * SCALE).astype(jnp.bfloat16) for part in parts], axis=1
        )
        shrink = jnp.exp2((highest - raised) * SCALE)
        top[rows, :] = raised
        gained = jnp.dot(weights, values[place], preferred_element_type=jnp.float32)
        acc[rows, :HD] = acc[rows, :HD] * shrink + gained[:, :HD]
        acc[rows, HD:] = acc[rows, HD:] * shrink + gained[:, HD:]

    def attend(places):
        last = 4 * places - 1
        score(0, 0, 0)

        def two(j, carried):
            i = 2 * j
            score((i + 1) // 4, (i + 1) % 4, 1)
            fold(i // 4, i % 4, 0)
            after = jnp.minimum(i + 2, last)
            score(after // 4, after % 4, 0)
            fold((i + 1) // 4, (i + 1) % 4, 1)
            return carried

        lax.fori_loop(0, 2 * places, two, 0)

    def collect(p):
        for ch in range(CHUNKS):
            for e in range(1, 4):
                hand_copy(p, ch, e).wait_recv()

    for h in range(4):
        query_copy(h).wait_recv()
    for ch in range(CHUNKS):
        hand_out(1, ch)
        hand_out(5, ch)
    collect(0)
    prepare(0, 0)
    attend(1)

    for i in range(4):
        bundle_wait(i).wait_recv()
        moved = pltpu.make_async_copy(near.at[i], near_s.at[i], smem_sem.at[1 + i])
        moved.start()
        moved.wait()

    def near_copy(d, ch, e):
        return remote(
            near_stage.at[d, ch, e],
            inbox.at[(3, 7)[d], ch, e],
            nsend.at[d, ch, e],
            nrecv.at[d, ch, e],
            device(e, up_down[d]),
        )

    def far_copy(d, ch):
        return remote(
            far_stage.at[d, ch],
            far_in.at[d, ch],
            fsend.at[d, ch],
            frecv.at[d, ch],
            device(0, up_down[d]),
        )

    def last_copy(d, ch, e):
        return remote(
            far_in.at[d, ch, e],
            inbox.at[4, ch, e, pl.ds(d * PIECE, PIECE)],
            gsend.at[d, ch, e],
            grecv.at[d, ch, e],
            device(e, up_down[d]),
        )

    for ch in range(CHUNKS):
        for d in range(2):
            ring(d, 2, ch).wait_recv()
            block = hop_bufs[d][1][ch]
            owner = yl * 16 + plane(-2 * up_down[d]) * 2 + c
            for e in range(4):
                far_stage[d, ch, e] = block[asked(near_s.at[2 * d + 1], e, owner, d)]
            far_copy(d, ch).start()
            for e in (3, 2, 1, 0):
                for rank in range(2):
                    slot = asked(near_s.at[2 * d], e, owner, rank)
                    near_stage[d, ch, e, pl.ds(rank * PIECE, PIECE), :] = block[slot]
                near_copy(d, ch, e).start()
        hand_out(2, ch)
        hand_out(6, ch)

    for place, p in enumerate((1, 5)):
        collect(p)
        prepare(p, place)
    attend(2)
    for d, ch in both:
        far_copy(d, ch).wait_recv()
        for e in (3, 2, 1, 0):
            last_copy(d, ch, e).start()
    for place, p in enumerate((2, 6)):
        collect(p)
        prepare(p, place)
    attend(2)
    for d, ch in both:
        for e in range(4):
            near_copy(d, ch, e).wait_recv()
    for place, p in enumerate((3, 7)):
        prepare(p, place)
    attend(2)
    for d, ch in both:
        for e in range(4):
            last_copy(d, ch, e).wait_recv()
    prepare(4, 0)

    def part_copy(i):
        return remote(part_out.at[i], part_in.at[i], osend.at[i], orecv.at[i], xid)

    def stat_copy(i):
        return remote(stat_out.at[i], stat_in.at[i], ssend.at[i], srecv.at[i], xid)

    def hand_back(i):
        base = (2 + i) * TILE
        part_out[i] = acc[pl.ds(base, TILE), :HD].astype(jnp.bfloat16)
        part_copy(i).start()
        for j in range(4):
            rows = pl.ds(base + j * HD, HD)
            stat_out[i, j : j + 1, :] = as_row(top[rows, :])
            stat_out[i, 4 + j : 5 + j, :] = as_row(acc[rows, HD:])
        stat_copy(i).start()

    score(0, 2, 0)
    score(0, 3, 1)
    fold(0, 2, 0)
    hand_back(0)
    score(0, 0, 0)
    fold(0, 3, 1)
    hand_back(1)
    score(0, 1, 1)
    fold(0, 0, 0)
    fold(0, 1, 1)

    for i in range(2):
        part_copy(i).wait_recv()
        stat_copy(i).wait_recv()
        for j in range(4):
            base = i * TILE + j * HD
            rows = pl.ds(base, HD)
            here = top[rows, :]
            there = jnp.broadcast_to(column(stat_in[i, j : j + 1, :]), (HD, HD))
            extra = jnp.broadcast_to(column(stat_in[i, 4 + j : 5 + j, :]), (HD, HD))
            peak = jnp.maximum(here, there)
            keep, take = jnp.exp2((here - peak) * SCALE), jnp.exp2((there - peak) * SCALE)
            sums = acc[rows, HD:] * keep + extra * take
            mixed = acc[rows, :HD] * keep + part_in[i, pl.ds(j * HD, HD), :].astype(
                jnp.float32
            ) * take
            span_out[pl.ds(base % 256, HD), pl.ds(base // 256 * HD, HD)] = (mixed / sums).astype(
                jnp.bfloat16
            )

    for d, ch in both:
        ring(d, 1, ch).wait_send()
        ring(d, 2, ch).wait_send()
        far_copy(d, ch).wait_send()
        for e in range(4):
            near_copy(d, ch, e).wait_send()
            last_copy(d, ch, e).wait_send()
    for i in range(4):
        bundle_copy(i).wait_send()
        query_copy(i).wait_send()
    for i in range(2):
        part_copy(i).wait_send()
        stat_copy(i).wait_send()
    for e in range(1, 4):
        table_copy(e).wait_send()
        for p in (0, 1, 2, 5, 6):
            for ch in range(CHUNKS):
                hand_copy(p, ch, e).wait_send()


def staged(*refs):
    first = 9 + 2 + 2
    flat = refs[first : first + 8]
    bufs = tuple(tuple(tuple(flat[(d * 2 + k) * 2 + ch] for ch in range(2)) for k in range(2)) for d in range(2))
    kernel(*refs[:first], bufs, *refs[first + 8 :])


def local(
    span_query,
    span_kv,
    kv_pool,
    hit_owner,
    hit_slot,
    decode_query,
    decode_kv,
    decode_table,
    decode_length,
):
    vmem = pl.BlockSpec(memory_space=pltpu.VMEM)
    smem = pl.BlockSpec(memory_space=pltpu.SMEM)
    hbm = pl.BlockSpec(memory_space=pl.ANY)
    dma = pltpu.SemaphoreType.DMA
    bf16, f32 = jnp.bfloat16, jnp.float32
    return pl.pallas_call(
        staged,
        out_shape=(
            jax.ShapeDtypeStruct(span_query.shape, bf16),
            jax.ShapeDtypeStruct(decode_query.shape, bf16),
        ),
        in_specs=[smem, smem, vmem, vmem, vmem, vmem, vmem, hbm, hbm],
        out_specs=(vmem, vmem),
        scratch_shapes=[
            pltpu.VMEM((16, 128, 256), bf16),
            pltpu.VMEM((2048, HD), bf16),
        ]
        + [pltpu.VMEM((16, PIECE, 256), bf16)] * 8
        + [
            pltpu.VMEM((5, CHUNKS, 4, 2 * PIECE, 256), bf16),
            pltpu.VMEM((2, CHUNKS, 4, 2 * PIECE, 256), bf16),
            pltpu.VMEM((2, CHUNKS, 4, PIECE, 256), bf16),
            pltpu.VMEM((2, CHUNKS, 4, PIECE, 256), bf16),
            pltpu.VMEM((NZ, CHUNKS, 4, 2 * PIECE, 256), bf16),
            pltpu.VMEM((4, 8, 128), jnp.int32),
            pltpu.SMEM((8, 128), jnp.int32),
            pltpu.VMEM((8, 128), jnp.int32),
            pltpu.VMEM((4, 8, 128), jnp.int32),
            pltpu.SMEM((4, 8, 128), jnp.int32),
            pltpu.VMEM((2, 512, HD), bf16),
            pltpu.VMEM((2, 512, 2 * HD), bf16),
            pltpu.VMEM((2, TILE, 512), f32),
            pltpu.VMEM((2048, 2 * HD), f32),
            pltpu.VMEM((2048, HD), f32),
            pltpu.VMEM((2, TILE, HD), bf16),
            pltpu.VMEM((2, TILE, HD), bf16),
            pltpu.VMEM((2, 8, 128), f32),
            pltpu.VMEM((2, 8, 128), f32),
            dma((5,)),
            dma((2, 2, CHUNKS)),
            dma((2, 2, CHUNKS)),
            dma((NZ, CHUNKS, 4)),
            dma((NZ, CHUNKS, 4)),
            dma((2, CHUNKS, 4)),
            dma((2, CHUNKS, 4)),
            dma((2, CHUNKS)),
            dma((2, CHUNKS)),
            dma((2, CHUNKS, 4)),
            dma((2, CHUNKS, 4)),
            dma((4,)),
            dma((4,)),
            dma((4,)),
            dma((4,)),
            dma((5,)),
            dma((4,)),
            dma((4,)),
            dma((2,)),
            dma((2,)),
            dma((2,)),
            dma((2,)),
        ],
        compiler_params=pltpu.CompilerParams(
            collective_id=0, has_side_effects=True, vmem_limit_bytes=56 * 1024 * 1024
        ),
        cost_estimate=pl.CostEstimate(
            flops=5 * 10**9, bytes_accessed=3 * 2**20, transcendentals=10**7
        ),
        name="spanned_attention",
    )(
        hit_owner.reshape(-1),
        hit_slot,
        decode_table.T,
        decode_length,
        decode_query,
        decode_kv,
        span_kv,
        span_query,
        kv_pool,
    )


def solution(mesh):
    placed = (
        P("replica", "tensor"),
        P("replica", "tensor"),
        P("replica", None, "tensor"),
        P("replica", None),
        P("replica"),
        P("replica", "tensor"),
        P("replica", "tensor"),
        P("replica", None),
        P("replica", None),
    )
    return jax.shard_map(
        local,
        mesh=mesh,
        in_specs=placed,
        out_specs=(P("replica", "tensor"), P("replica", "tensor")),
        check_vma=False,
    )
```

time: 82.2 us -> 68.2 us (0.83)
  Pallas kernels: 79.1 us -> 65.1 us
    pallas_call x1, Pallas kernels: 79.1 us -> 65.1 us  [local(): pl.pallas_call(staged, out_shape=(jax.ShapeDtypeStruct(span_query.shape,...]
where the time goes in v2:
time: 68.2 us; the launch traced here: 68.1 us
  Pallas kernels  65.1 us (95%)
  local copies, waits for them, and re-layouts  2.29 us (3%)
    pallas_call x1, Pallas kernels, local(): pl.pallas_call(staged, out_shape=(jax.ShapeDtypeStruct(span_query.shape,...  65.1 us
    unnamed x4, local copies, waits for them, and re-layouts  2.29 us

profile of v2, /device:TPU:16, one launch (start us, length us, event | category | flops | bytes accessed | tf_op | source)
XLA Modules:
  0.0 68.1 jit_solution(3089264451114423217)
XLA Ops:
  0.6 65.1 %spanned_attention.1 = (bf16[256,512]{1,0:T(8,128)(2,1)}, bf16[32,512]{1,0:T(8,128)(2,1)}) custom-call(s32[32]{0:T(128)} %bitcast.3, s32[32]{0:T(128)} %refs_1_.1, s32[4,32]{1,0:T(4,128)} %bitcast.2, s32[1,32]{1,0:T(1,128)} %refs_3_.1, bf16[32,512]{1,0:T(8,128)(2,1)} %refs_4_.1, bf16[32,256]{1,0:T(8,128)(2,1)} %refs_5_.1, bf16[256,256]{1,0:T(8,128)(2,1)} %refs_6_.1, ...), custom_call_target="tpu_custom_call" | custom-call | flops 5000000000 | bytes 3145728 | tf_op jit(solution)/shard_map/spanned_attention/pallas_call | solution.py:571
  65.8 0.0 copy-start
  65.8 1.7 %copy.13 = bf16[256,512]{1,0:T(8,128)(2,1)} copy(bf16[256,512]{1,0:T(8,128)(2,1)} %get-tuple-element.4) | data formatting | bytes 524288
  67.5 0.0 copy-done
  67.5 0.6 copy.14
Async XLA Ops:
  65.8 1.7 %copy-start = (bf16[32,512]{1,0:T(8,128)(2,1)S(1)}, bf16[32,512]{1,0:T(8,128)(2,1)}, u32[]{:S(2)}) copy-start(bf16[32,512]{1,0:T(8,128)(2,1)} %get-tuple-element.5) | copy-start | bytes 98308

commit v3 on v2

--- a/solution.py
+++ b/solution.py
@@ -37,6 +37,17 @@
 
 
 def kernel(
+    owner_hbm,
+    slot_hbm,
+    table_hbm,
+    length_hbm,
+    dq_hbm,
+    dkv_hbm,
+    skv_hbm,
+    q_hbm,
+    pool_hbm,
+    span_hbm,
+    decode_hbm,
     owner_s,
     slot_s,
     table_ref,
@@ -44,8 +55,6 @@
     dq_ref,
     dkv_ref,
     skv_ref,
-    q_hbm,
-    pool_hbm,
     span_out,
     decode_out,
     pool_v,
@@ -71,6 +80,7 @@
     stat_out,
     stat_in,
     load_sem,
+    store_sem,
     zsend,
     zrecv,
     psend,
@@ -119,15 +129,19 @@
     for other in partners:
         pl.semaphore_signal(barrier, inc=1, device_id=other, device_id_type=MESH)
 
-    loads = [pltpu.make_async_copy(pool_hbm, pool_v, load_sem.at[0])]
+    pairs = [
+        (owner_hbm, owner_s),
+        (slot_hbm, slot_s),
+        (pool_hbm, pool_v),
+        (table_hbm, table_ref),
+        (length_hbm, length_ref),
+        (dq_hbm, dq_ref),
+        (dkv_hbm, dkv_ref),
+        (skv_hbm, skv_ref),
+    ]
     for h in range(4):
-        loads.append(
-            pltpu.make_async_copy(
-                q_hbm.at[:, pl.ds(h * HD, HD)], qall.at[pl.ds(h * 256, 256)], load_sem.at[1 + h]
-            )
-        )
-    for copy in loads:
-        copy.start()
+        pairs.append((q_hbm.at[:, pl.ds(h * HD, HD)], qall.at[pl.ds(h * 256, 256)]))
+    loads = [pltpu.make_async_copy(src, dst, load_sem.at[i]) for i, (src, dst) in enumerate(pairs)]
 
     def remote(src, dst, send, recv, where):
         return pltpu.make_async_remote_copy(
@@ -158,6 +172,8 @@
     pl.semaphore_wait(barrier, len(partners))
     for d, ch in both:
         ring(d, 1, ch).start()
+    for copy in loads:
+        copy.start()
 
     def query_copy(h):
         return remote(
@@ -168,6 +184,9 @@
             xid,
         )
 
+    for copy in loads[:2]:
+        copy.wait()
+
     lane = lax.broadcasted_iota(jnp.int32, (8, 128), 1)
     lane_owner, lane_rank = lane // 2, lane % 2
 
@@ -192,6 +211,50 @@
         table_copy(e).start()
     for h in range(4):
         query_copy(h).start()
+
+    for copy in loads[2:7]:
+        copy.wait()
+    count = 32
+    dq = jnp.concatenate([dq_ref[:, pl.ds(g * HD, HD)] for g in range(4)], axis=0)
+    lengths = column(length_ref[...].astype(jnp.float32))
+    names = [column(table_ref[b : b + 1, :].astype(jnp.float32)) for b in range(4)]
+    spot = lax.broadcasted_iota(jnp.int32, (count, HD), 1).astype(jnp.float32)
+
+    def times(block):
+        seen = jnp.zeros((count, HD), jnp.float32)
+        for b in range(4):
+            limit = jnp.where(names[b] == block, lengths - 128.0 * b, 0.0)
+            seen = seen + jnp.where(spot < limit, 1.0, 0.0)
+        return jnp.concatenate([seen] * 4, axis=0)
+
+    own_key = jnp.concatenate([dkv_ref[:, :HD].astype(jnp.float32)] * 4, axis=0)
+    own_value = jnp.concatenate([dkv_ref[:, HD:].astype(jnp.float32)] * 4, axis=0)
+    own_score = jnp.sum(dq.astype(jnp.float32) * own_key, axis=1, keepdims=True)
+
+    def decode_step(it, carried):
+        highest, weight_sum, mixture = carried
+        rows = pool_v[pl.ds(it * 4, 4)].reshape(4 * HD, 2 * HD)
+        scores = nt_dot(dq, rows[:, :HD])
+        seen = jnp.concatenate([times((it * 4 + i).astype(jnp.float32)) for i in range(4)], axis=1)
+        masked = jnp.where(seen > 0.0, scores, LOW)
+        raised = jnp.maximum(highest, jnp.max(masked, axis=1, keepdims=True))
+        weights = jnp.exp2((masked - raised) * SCALE)
+        shrink = jnp.exp2((highest - raised) * SCALE)
+        weight_sum = weight_sum * shrink + jnp.sum(weights * seen, axis=1, keepdims=True)
+        spread = (weights.astype(jnp.bfloat16).astype(jnp.float32) * seen).astype(jnp.bfloat16)
+        mixture = mixture * shrink + jnp.dot(
+            spread, rows[:, HD:], preferred_element_type=jnp.float32
+        )
+        return raised, weight_sum, mixture
+
+    _, weight_sum, mixture = lax.fori_loop(
+        0, 4, decode_step, (own_score, jnp.ones((128, 1), jnp.float32), own_value)
+    )
+    mixed = (mixture / weight_sum).astype(jnp.bfloat16)
+    for g in range(4):
+        decode_out[:, pl.ds(g * HD, HD)] = mixed[g * count : (g + 1) * count]
+    decoded = pltpu.make_async_copy(decode_out, decode_hbm, store_sem.at[0])
+    decoded.start()
 
     steps = (1, 2, -1, -2)
 
@@ -211,7 +274,6 @@
         bundle_copy(i).start()
     moved = pltpu.make_async_copy(bundle, tabs_s, smem_sem.at[0])
     moved.start()
-    loads[0].wait()
     moved.wait()
 
     def plane_of(p):
@@ -251,54 +313,16 @@
     for ch in range(CHUNKS):
         hand_out(0, ch)
 
-    count = 32
-    dq = jnp.concatenate([dq_ref[:, pl.ds(g * HD, HD)] for g in range(4)], axis=0)
-    lengths = column(length_ref[...].astype(jnp.float32))
-    names = [column(table_ref[b : b + 1, :].astype(jnp.float32)) for b in range(4)]
-    spot = lax.broadcasted_iota(jnp.int32, (count, HD), 1).astype(jnp.float32)
-
-    def times(block):
-        seen = jnp.zeros((count, HD), jnp.float32)
-        for b in range(4):
-            limit = jnp.where(names[b] == block, lengths - 128.0 * b, 0.0)
-            seen = seen + jnp.where(spot < limit, 1.0, 0.0)
-        return jnp.concatenate([seen] * 4, axis=0)
-
-    own_key = jnp.concatenate([dkv_ref[:, :HD].astype(jnp.float32)] * 4, axis=0)
-    own_value = jnp.concatenate([dkv_ref[:, HD:].astype(jnp.float32)] * 4, axis=0)
-    own_score = jnp.sum(dq.astype(jnp.float32) * own_key, axis=1, keepdims=True)
-
-    def decode_step(it, carried):
-        highest, weight_sum, mixture = carried
-        rows = pool_v[pl.ds(it * 4, 4)].reshape(4 * HD, 2 * HD)
-        scores = nt_dot(dq, rows[:, :HD])
-        seen = jnp.concatenate([times((it * 4 + i).astype(jnp.float32)) for i in range(4)], axis=1)
-        masked = jnp.where(seen > 0.0, scores, LOW)
-        raised = jnp.maximum(highest, jnp.max(masked, axis=1, keepdims=True))
-        weights = jnp.exp2((masked - raised) * SCALE)
-        shrink = jnp.exp2((highest - raised) * SCALE)
-        weight_sum = weight_sum * shrink + jnp.sum(weights * seen, axis=1, keepdims=True)
-        spread = (weights.astype(jnp.bfloat16).astype(jnp.float32) * seen).astype(jnp.bfloat16)
-        mixture = mixture * shrink + jnp.dot(
-            spread, rows[:, HD:], preferred_element_type=jnp.float32
-        )
-        return raised, weight_sum, mixture
-
-    _, weight_sum, mixture = lax.fori_loop(
-        0, 4, decode_step, (own_score, jnp.ones((128, 1), jnp.float32), own_value)
-    )
-    mixed = (mixture / weight_sum).astype(jnp.bfloat16)
-    for g in range(4):
-        decode_out[:, pl.ds(g * HD, HD)] = mixed[g * count : (g + 1) * count]
-
     def forward(ch):
         for d in range(2):
             ring(d, 1, ch).wait_recv()
             ring(d, 2, ch).start()
 
     forward(0)
-
-    for copy in loads[1:]:
+    hand_out(1, 0)
+    hand_out(5, 0)
+
+    for copy in loads[7:]:
         copy.wait()
     fresh_keys = skv_ref[:, :HD]
     fresh_values = jnp.concatenate([skv_ref[:, HD:], jnp.ones((256, HD), jnp.bfloat16)], axis=1)
@@ -329,20 +353,22 @@
 
     lax.fori_loop(0, 2, fresh_step, 0)
     forward(1)
+    hand_out(1, 1)
+    hand_out(5, 1)
 
     seen_key = jnp.broadcast_to(skv_ref[0:1, :HD].astype(jnp.float32), (PIECE, HD)).astype(
         jnp.bfloat16
     )
 
-    def prepare(p, place):
-        for ch in range(CHUNKS):
+    def prepare(unit, place):
+        for i, (p, ch) in enumerate(unit):
             for e in range(4):
                 py, pc = peer(e)
                 owner = py * 16 + plane_of(p) * 2 + pc
                 for rank in range(2):
                     used = tabs_s[0, owner * 2 + rank] >= 0
                     cell = inbox[p, ch, e, pl.ds(rank * PIECE, PIECE), :]
-                    rows = pl.ds(((ch * 4 + e) * 2 + rank) * PIECE, PIECE)
+                    rows = pl.ds(((i * 4 + e) * 2 + rank) * PIECE, PIECE)
                     keys[place, rows, :] = jnp.where(used, cell[:, :HD], seen_key)
                     values[place, rows, :HD] = jnp.where(
                         used, cell[:, HD:], jnp.zeros((PIECE, HD), jnp.bfloat16)
@@ -353,6 +379,9 @@
                         jnp.zeros((PIECE, HD), jnp.bfloat16),
                     )
 
+    def whole(p):
+        return [(p, ch) for ch in range(CHUNKS)]
+
     def tile_rows(tile):
         if isinstance(tile, int):
             return pl.ds(tile * TILE, TILE)
@@ -393,18 +422,17 @@
 
         lax.fori_loop(0, 2 * places, two, 0)
 
-    def collect(p):
-        for ch in range(CHUNKS):
+    both_chunks = tuple(range(CHUNKS))
+
+    def collect(p, chunks):
+        for ch in chunks:
             for e in range(1, 4):
                 hand_copy(p, ch, e).wait_recv()
 
     for h in range(4):
         query_copy(h).wait_recv()
-    for ch in range(CHUNKS):
-        hand_out(1, ch)
-        hand_out(5, ch)
-    collect(0)
-    prepare(0, 0)
+    collect(0, both_chunks)
+    prepare(whole(0), 0)
     attend(1)
 
     for i in range(4):
@@ -440,7 +468,7 @@
             device(e, up_down[d]),
         )
 
-    for ch in range(CHUNKS):
+    def send_far(ch):
         for d in range(2):
             ring(d, 2, ch).wait_recv()
             block = hop_bufs[d][1][ch]
@@ -448,36 +476,58 @@
             for e in range(4):
                 far_stage[d, ch, e] = block[asked(near_s.at[2 * d + 1], e, owner, d)]
             far_copy(d, ch).start()
+
+    def send_near(ch):
+        for d in range(2):
+            block = hop_bufs[d][1][ch]
+            owner = yl * 16 + plane(-2 * up_down[d]) * 2 + c
             for e in (3, 2, 1, 0):
                 for rank in range(2):
                     slot = asked(near_s.at[2 * d], e, owner, rank)
                     near_stage[d, ch, e, pl.ds(rank * PIECE, PIECE), :] = block[slot]
                 near_copy(d, ch, e).start()
-        hand_out(2, ch)
-        hand_out(6, ch)
-
+
+    send_far(0)
+    send_near(0)
+    hand_out(2, 0)
+    hand_out(6, 0)
     for place, p in enumerate((1, 5)):
-        collect(p)
-        prepare(p, place)
+        collect(p, both_chunks)
+        prepare(whole(p), place)
     attend(2)
-    for d, ch in both:
-        far_copy(d, ch).wait_recv()
-        for e in (3, 2, 1, 0):
-            last_copy(d, ch, e).start()
-    for place, p in enumerate((2, 6)):
-        collect(p)
-        prepare(p, place)
-    attend(2)
-    for d, ch in both:
-        for e in range(4):
-            near_copy(d, ch, e).wait_recv()
-    for place, p in enumerate((3, 7)):
-        prepare(p, place)
-    attend(2)
+    send_far(1)
+    send_near(1)
+    hand_out(2, 1)
+    hand_out(6, 1)
+
+    def forward_far(ch):
+        for d in range(2):
+            far_copy(d, ch).wait_recv()
+            for e in (3, 2, 1, 0):
+                last_copy(d, ch, e).start()
+
+    def pair_unit(p, ch):
+        unit = [(p, ch), (p + 4, ch)]
+        if p < 3:
+            for q, _ in unit:
+                collect(q, (ch,))
+        else:
+            for d in range(2):
+                for e in range(4):
+                    near_copy(d, ch, e).wait_recv()
+        prepare(unit, 0)
+        attend(1)
+
+    forward_far(0)
+    pair_unit(2, 0)
+    forward_far(1)
+    pair_unit(2, 1)
+    pair_unit(3, 0)
+    pair_unit(3, 1)
     for d, ch in both:
         for e in range(4):
             last_copy(d, ch, e).wait_recv()
-    prepare(4, 0)
+    prepare(whole(4), 0)
 
     def part_copy(i):
         return remote(part_out.at[i], part_in.at[i], osend.at[i], orecv.at[i], xid)
@@ -506,6 +556,7 @@
     fold(0, 0, 0)
     fold(0, 1, 1)
 
+    stored = [decoded]
     for i in range(2):
         part_copy(i).wait_recv()
         stat_copy(i).wait_recv()
@@ -524,6 +575,16 @@
             span_out[pl.ds(base % 256, HD), pl.ds(base // 256 * HD, HD)] = (mixed / sums).astype(
                 jnp.bfloat16
             )
+            if j % 2:
+                h = 2 * i + j // 2
+                stored.append(
+                    pltpu.make_async_copy(
+                        span_out.at[:, pl.ds(h * HD, HD)],
+                        span_hbm.at[:, pl.ds(h * HD, HD)],
+                        store_sem.at[1 + h],
+                    )
+                )
+                stored[-1].start()
 
     for d, ch in both:
         ring(d, 1, ch).wait_send()
@@ -543,13 +604,20 @@
         for p in (0, 1, 2, 5, 6):
             for ch in range(CHUNKS):
                 hand_copy(p, ch, e).wait_send()
+    for copy in stored:
+        copy.wait()
 
 
 def staged(*refs):
-    first = 9 + 2 + 2
+    first = 9 + 2 + 9 + 2
     flat = refs[first : first + 8]
     bufs = tuple(tuple(tuple(flat[(d * 2 + k) * 2 + ch] for ch in range(2)) for k in range(2)) for d in range(2))
     kernel(*refs[:first], bufs, *refs[first + 8 :])
+
+
+def place_results(span_ref, decode_ref, span_out, decode_out):
+    span_out[...] = span_ref[...]
+    decode_out[...] = decode_ref[...]
 
 
 def local(
@@ -563,20 +631,27 @@
     decode_table,
     decode_length,
 ):
-    vmem = pl.BlockSpec(memory_space=pltpu.VMEM)
-    smem = pl.BlockSpec(memory_space=pltpu.SMEM)
     hbm = pl.BlockSpec(memory_space=pl.ANY)
     dma = pltpu.SemaphoreType.DMA
     bf16, f32 = jnp.bfloat16, jnp.float32
-    return pl.pallas_call(
+    results = pl.pallas_call(
         staged,
         out_shape=(
             jax.ShapeDtypeStruct(span_query.shape, bf16),
             jax.ShapeDtypeStruct(decode_query.shape, bf16),
         ),
-        in_specs=[smem, smem, vmem, vmem, vmem, vmem, vmem, hbm, hbm],
-        out_specs=(vmem, vmem),
+        in_specs=[hbm] * 9,
+        out_specs=(hbm, hbm),
         scratch_shapes=[
+            pltpu.SMEM((32,), jnp.int32),
+            pltpu.SMEM((32,), jnp.int32),
+            pltpu.VMEM((4, 32), jnp.int32),
+            pltpu.VMEM((1, 32), jnp.int32),
+            pltpu.VMEM(decode_query.shape, bf16),
+            pltpu.VMEM(decode_kv.shape, bf16),
+            pltpu.VMEM(span_kv.shape, bf16),
+            pltpu.VMEM(span_query.shape, bf16),
+            pltpu.VMEM(decode_query.shape, bf16),
             pltpu.VMEM((16, 128, 256), bf16),
             pltpu.VMEM((2048, HD), bf16),
         ]
@@ -601,6 +676,7 @@
             pltpu.VMEM((2, TILE, HD), bf16),
             pltpu.VMEM((2, 8, 128), f32),
             pltpu.VMEM((2, 8, 128), f32),
+            dma((12,)),
             dma((5,)),
             dma((2, 2, CHUNKS)),
             dma((2, 2, CHUNKS)),
@@ -642,6 +718,17 @@
         span_query,
         kv_pool,
     )
+    vmem = pl.BlockSpec(memory_space=pltpu.VMEM)
+    return pl.pallas_call(
+        place_results,
+        out_shape=(
+            jax.ShapeDtypeStruct(span_query.shape, bf16),
+            jax.ShapeDtypeStruct(decode_query.shape, bf16),
+        ),
+        in_specs=[vmem] * 2,
+        out_specs=(vmem,) * 2,
+        name="place_results",
+    )(*results)
 
 
 def solution(mesh):

time: 68.2 us -> 65.4 us (0.959)
  the two profiles are of different devices: /device:TPU:16 before, /device:TPU:32 now
where the time goes in v3:
time: 65.4 us; the launch traced here: 65.2 us
  Pallas kernels  64.6 us (99%)
    pallas_call x1, Pallas kernels, local(): pl.pallas_call(staged, out_shape=(jax.ShapeDtypeStruct(span_query.shape,...  62.9 us
    pallas_call x1, Pallas kernels, local(): pl.pallas_call(place_results, out_shape=(jax.ShapeDtypeStruct(span_query....  1.68 us

profile of v3, /device:TPU:32, one launch (start us, length us, event | category | flops | bytes accessed | tf_op | source)
XLA Modules:
  0.0 65.2 jit_solution(3950041746187249189)
XLA Ops:
  0.6 62.9 %spanned_attention.1 = (bf16[256,512]{1,0:T(8,128)(2,1)}, bf16[32,512]{1,0:T(8,128)(2,1)}) custom-call(s32[32]{0:T(128)} %bitcast.3, s32[32]{0:T(128)} %refs_1_.1, s32[4,32]{1,0:T(4,128)} %bitcast.2, s32[1,32]{1,0:T(1,128)} %refs_3_.1, bf16[32,512]{1,0:T(8,128)(2,1)} %refs_4_.1, bf16[32,256]{1,0:T(8,128)(2,1)} %refs_5_.1, bf16[256,256]{1,0:T(8,128)(2,1)} %refs_6_.1, ...), custom_call_target="tpu_custom_call" | custom-call | flops 5000000000 | bytes 3145728 | tf_op jit(solution)/shard_map/spanned_attention/pallas_call | solution.py:637
  63.6 1.7 %place_results.1 = (bf16[256,512]{1,0:T(8,128)(2,1)}, bf16[32,512]{1,0:T(8,128)(2,1)}) custom-call(bf16[256,512]{1,0:T(8,128)(2,1)} %get-tuple-element.4.span_ref, bf16[32,512]{1,0:T(8,128)(2,1)} %get-tuple-element.5.decode_ref), custom_call_target="tpu_custom_call" | custom-call | tf_op jit(solution)/shard_map/place_results/pallas_call | solution.py:722

commit v4 on v3

--- a/solution.py
+++ b/solution.py
@@ -506,7 +506,7 @@
             for e in (3, 2, 1, 0):
                 last_copy(d, ch, e).start()
 
-    def pair_unit(p, ch):
+    def pair_unit(p, ch, theirs=False):
         unit = [(p, ch), (p + 4, ch)]
         if p < 3:
             for q, _ in unit:
@@ -516,18 +516,24 @@
                 for e in range(4):
                     near_copy(d, ch, e).wait_recv()
         prepare(unit, 0)
-        attend(1)
+        if theirs:
+            score(0, 2, 0)
+            score(0, 3, 1)
+            fold(0, 2, 0)
+            fold(0, 3, 1)
+        else:
+            attend(1)
 
     forward_far(0)
     pair_unit(2, 0)
     forward_far(1)
     pair_unit(2, 1)
     pair_unit(3, 0)
-    pair_unit(3, 1)
+    pair_unit(3, 1, True)
     for d, ch in both:
         for e in range(4):
             last_copy(d, ch, e).wait_recv()
-    prepare(whole(4), 0)
+    prepare(whole(4), 1)
 
     def part_copy(i):
         return remote(part_out.at[i], part_in.at[i], osend.at[i], orecv.at[i], xid)
@@ -545,17 +551,36 @@
             stat_out[i, 4 + j : 5 + j, :] = as_row(acc[rows, HD:])
         stat_copy(i).start()
 
-    score(0, 2, 0)
-    score(0, 3, 1)
-    fold(0, 2, 0)
+    score(1, 2, 0)
+    score(1, 3, 1)
+    fold(1, 2, 0)
     hand_back(0)
     score(0, 0, 0)
-    fold(0, 3, 1)
+    fold(1, 3, 1)
     hand_back(1)
     score(0, 1, 1)
     fold(0, 0, 0)
+    score(1, 0, 0)
     fold(0, 1, 1)
-
+    score(1, 1, 1)
+    fold(1, 0, 0)
+    fold(1, 1, 1)
+
+    for d, ch in both:
+        ring(d, 1, ch).wait_send()
+        ring(d, 2, ch).wait_send()
+        far_copy(d, ch).wait_send()
+        for e in range(4):
+            near_copy(d, ch, e).wait_send()
+            last_copy(d, ch, e).wait_send()
+    for i in range(4):
+        bundle_copy(i).wait_send()
+        query_copy(i).wait_send()
+    for e in range(1, 4):
+        table_copy(e).wait_send()
+        for p in (0, 1, 2, 5, 6):
+            for ch in range(CHUNKS):
+                hand_copy(p, ch, e).wait_send()
     stored = [decoded]
     for i in range(2):
         part_copy(i).wait_recv()
@@ -586,24 +611,9 @@
                 )
                 stored[-1].start()
 
-    for d, ch in both:
-        ring(d, 1, ch).wait_send()
-        ring(d, 2, ch).wait_send()
-        far_copy(d, ch).wait_send()
-        for e in range(4):
-            near_copy(d, ch, e).wait_send()
-            last_copy(d, ch, e).wait_send()
-    for i in range(4):
-        bundle_copy(i).wait_send()
-        query_copy(i).wait_send()
     for i in range(2):
         part_copy(i).wait_send()
         stat_copy(i).wait_send()
-    for e in range(1, 4):
-        table_copy(e).wait_send()
-        for p in (0, 1, 2, 5, 6):
-            for ch in range(CHUNKS):
-                hand_copy(p, ch, e).wait_send()
     for copy in stored:
         copy.wait()
 

time: 65.4 us -> 64.3 us (0.983)
  Pallas kernels: 64.6 us -> 63.5 us
    pallas_call x1, Pallas kernels: 62.9 us -> 61.8 us  [local(): pl.pallas_call(staged, out_shape=(jax.ShapeDtypeStruct(span_query.shape,...]
where the time goes in v4:
time: 64.3 us; the launch traced here: 64.1 us
  Pallas kernels  63.5 us (99%)
    pallas_call x1, Pallas kernels, local(): pl.pallas_call(staged, out_shape=(jax.ShapeDtypeStruct(span_query.shape,...  61.8 us
    pallas_call x1, Pallas kernels, local(): pl.pallas_call(place_results, out_shape=(jax.ShapeDtypeStruct(span_query....  1.68 us

profile of v4, /device:TPU:32, one launch (start us, length us, event | category | flops | bytes accessed | tf_op | source)
XLA Modules:
  0.0 64.1 jit_solution(12489302384554166746)
XLA Ops:
  0.6 61.8 %spanned_attention.1 = (bf16[256,512]{1,0:T(8,128)(2,1)}, bf16[32,512]{1,0:T(8,128)(2,1)}) custom-call(s32[32]{0:T(128)} %bitcast.3, s32[32]{0:T(128)} %refs_1_.1, s32[4,32]{1,0:T(4,128)} %bitcast.2, s32[1,32]{1,0:T(1,128)} %refs_3_.1, bf16[32,512]{1,0:T(8,128)(2,1)} %refs_4_.1, bf16[32,256]{1,0:T(8,128)(2,1)} %refs_5_.1, bf16[256,256]{1,0:T(8,128)(2,1)} %refs_6_.1, ...), custom_call_target="tpu_custom_call" | custom-call | flops 5000000000 | bytes 3145728 | tf_op jit(solution)/shard_map/spanned_attention/pallas_call | solution.py:647
  62.5 1.7 %place_results.1 = (bf16[256,512]{1,0:T(8,128)(2,1)}, bf16[32,512]{1,0:T(8,128)(2,1)}) custom-call(bf16[256,512]{1,0:T(8,128)(2,1)} %get-tuple-element.4.span_ref, bf16[32,512]{1,0:T(8,128)(2,1)} %get-tuple-element.5.decode_ref), custom_call_target="tpu_custom_call" | custom-call | tf_op jit(solution)/shard_map/place_results/pallas_call | solution.py:732

commit v5 on v4

--- a/solution.py
+++ b/solution.py
@@ -62,6 +62,8 @@
     hop_bufs,
     stage,
     near_stage,
+    wide_stage,
+    wide_in,
     far_stage,
     far_in,
     inbox,
@@ -452,30 +454,50 @@
 
     def far_copy(d, ch):
         return remote(
-            far_stage.at[d, ch],
-            far_in.at[d, ch],
+            (wide_stage, far_stage)[ch].at[d],
+            (wide_in, far_in)[ch].at[d],
             fsend.at[d, ch],
             frecv.at[d, ch],
             device(0, up_down[d]),
         )
 
     def last_copy(d, ch, e):
+        place = inbox.at[4, ch, e] if ch == 0 else inbox.at[4, ch, e, pl.ds(d * PIECE, PIECE)]
         return remote(
-            far_in.at[d, ch, e],
-            inbox.at[4, ch, e, pl.ds(d * PIECE, PIECE)],
+            (wide_in, far_in)[ch].at[d, e],
+            place,
             gsend.at[d, ch, e],
             grecv.at[d, ch, e],
             device(e, up_down[d]),
         )
+
+    def on_way(d, hops):
+        first = (z - hops * up_down[d] + NZ) % NZ
+        return (first < 4) if d == 0 else (first >= 4)
+
+    def if_used(d, ch, hops, do):
+        if ch == 0:
+            pl.when(on_way(d, hops))(do)
+        else:
+            do()
 
     def send_far(ch):
         for d in range(2):
             ring(d, 2, ch).wait_recv()
             block = hop_bufs[d][1][ch]
             owner = yl * 16 + plane(-2 * up_down[d]) * 2 + c
-            for e in range(4):
-                far_stage[d, ch, e] = block[asked(near_s.at[2 * d + 1], e, owner, d)]
-            far_copy(d, ch).start()
+
+            def send(d=d, block=block, owner=owner):
+                for e in range(4):
+                    if ch == 0:
+                        for rank in range(2):
+                            slot = asked(near_s.at[2 * d + 1], e, owner, rank)
+                            wide_stage[d, e, pl.ds(rank * PIECE, PIECE), :] = block[slot]
+                    else:
+                        far_stage[d, e] = block[asked(near_s.at[2 * d + 1], e, owner, d)]
+                far_copy(d, ch).start()
+
+            if_used(d, ch, 2, send)
 
     def send_near(ch):
         for d in range(2):
@@ -487,24 +509,15 @@
                     near_stage[d, ch, e, pl.ds(rank * PIECE, PIECE), :] = block[slot]
                 near_copy(d, ch, e).start()
 
-    send_far(0)
-    send_near(0)
-    hand_out(2, 0)
-    hand_out(6, 0)
-    for place, p in enumerate((1, 5)):
-        collect(p, both_chunks)
-        prepare(whole(p), place)
-    attend(2)
-    send_far(1)
-    send_near(1)
-    hand_out(2, 1)
-    hand_out(6, 1)
-
     def forward_far(ch):
         for d in range(2):
-            far_copy(d, ch).wait_recv()
-            for e in (3, 2, 1, 0):
-                last_copy(d, ch, e).start()
+
+            def pass_on(d=d):
+                far_copy(d, ch).wait_recv()
+                for e in (3, 2, 1, 0):
+                    last_copy(d, ch, e).start()
+
+            if_used(d, ch, 3, pass_on)
 
     def pair_unit(p, ch, theirs=False):
         unit = [(p, ch), (p + 4, ch)]
@@ -524,6 +537,16 @@
         else:
             attend(1)
 
+    pair_unit(1, 0)
+    send_far(0)
+    send_near(0)
+    hand_out(2, 0)
+    hand_out(6, 0)
+    send_far(1)
+    send_near(1)
+    hand_out(2, 1)
+    hand_out(6, 1)
+    pair_unit(1, 1)
     forward_far(0)
     pair_unit(2, 0)
     forward_far(1)
@@ -531,33 +554,40 @@
     pair_unit(3, 0)
     pair_unit(3, 1, True)
     for d, ch in both:
-        for e in range(4):
-            last_copy(d, ch, e).wait_recv()
+
+        def arrive(d=d, ch=ch):
+            for e in range(4):
+                last_copy(d, ch, e).wait_recv()
+
+        if_used(d, ch, 4, arrive)
     prepare(whole(4), 1)
 
     def part_copy(i):
         return remote(part_out.at[i], part_in.at[i], osend.at[i], orecv.at[i], xid)
 
-    def stat_copy(i):
-        return remote(stat_out.at[i], stat_in.at[i], ssend.at[i], srecv.at[i], xid)
-
-    def hand_back(i):
-        base = (2 + i) * TILE
-        part_out[i] = acc[pl.ds(base, TILE), :HD].astype(jnp.bfloat16)
+    def stat_copy():
+        return remote(stat_out, stat_in, ssend.at[0], srecv.at[0], xid)
+
+    def send_part(i):
+        part_out[i] = acc[pl.ds((2 + i) * TILE, TILE), :HD].astype(jnp.bfloat16)
         part_copy(i).start()
-        for j in range(4):
-            rows = pl.ds(base + j * HD, HD)
-            stat_out[i, j : j + 1, :] = as_row(top[rows, :])
-            stat_out[i, 4 + j : 5 + j, :] = as_row(acc[rows, HD:])
-        stat_copy(i).start()
+
+    def send_stats():
+        for i in range(2):
+            for j in range(4):
+                rows = pl.ds((2 + i) * TILE + j * HD, HD)
+                stat_out[i, j : j + 1, :] = as_row(top[rows, :])
+                stat_out[i, 4 + j : 5 + j, :] = as_row(acc[rows, HD:])
+        stat_copy().start()
 
     score(1, 2, 0)
     score(1, 3, 1)
     fold(1, 2, 0)
-    hand_back(0)
+    send_part(0)
     score(0, 0, 0)
     fold(1, 3, 1)
-    hand_back(1)
+    send_stats()
+    send_part(1)
     score(0, 1, 1)
     fold(0, 0, 0)
     score(1, 0, 0)
@@ -569,10 +599,18 @@
     for d, ch in both:
         ring(d, 1, ch).wait_send()
         ring(d, 2, ch).wait_send()
-        far_copy(d, ch).wait_send()
         for e in range(4):
             near_copy(d, ch, e).wait_send()
-            last_copy(d, ch, e).wait_send()
+
+        def sent(d=d, ch=ch):
+            far_copy(d, ch).wait_send()
+
+        def passed(d=d, ch=ch):
+            for e in range(4):
+                last_copy(d, ch, e).wait_send()
+
+        if_used(d, ch, 2, sent)
+        if_used(d, ch, 3, passed)
     for i in range(4):
         bundle_copy(i).wait_send()
         query_copy(i).wait_send()
@@ -582,38 +620,38 @@
             for ch in range(CHUNKS):
                 hand_copy(p, ch, e).wait_send()
     stored = [decoded]
+    stat_copy().wait_recv()
     for i in range(2):
-        part_copy(i).wait_recv()
-        stat_copy(i).wait_recv()
         for j in range(4):
-            base = i * TILE + j * HD
-            rows = pl.ds(base, HD)
+            rows = pl.ds(i * TILE + j * HD, HD)
             here = top[rows, :]
             there = jnp.broadcast_to(column(stat_in[i, j : j + 1, :]), (HD, HD))
             extra = jnp.broadcast_to(column(stat_in[i, 4 + j : 5 + j, :]), (HD, HD))
             peak = jnp.maximum(here, there)
             keep, take = jnp.exp2((here - peak) * SCALE), jnp.exp2((there - peak) * SCALE)
-            sums = acc[rows, HD:] * keep + extra * take
-            mixed = acc[rows, :HD] * keep + part_in[i, pl.ds(j * HD, HD), :].astype(
-                jnp.float32
-            ) * take
-            span_out[pl.ds(base % 256, HD), pl.ds(base // 256 * HD, HD)] = (mixed / sums).astype(
-                jnp.bfloat16
+            inverse = 1.0 / (acc[rows, HD:] * keep + extra * take)
+            acc[rows, :HD] = acc[rows, :HD] * (keep * inverse)
+            top[rows, :] = take * inverse
+    for h in range(4):
+        if h % 2 == 0:
+            part_copy(h // 2).wait_recv()
+        rows = pl.ds(h * 256, 256)
+        other = part_in[h // 2, pl.ds(h % 2 * 256, 256), :].astype(jnp.float32)
+        span_out[:, pl.ds(h * HD, HD)] = (acc[rows, :HD] + other * top[rows, :]).astype(
+            jnp.bfloat16
+        )
+        stored.append(
+            pltpu.make_async_copy(
+                span_out.at[:, pl.ds(h * HD, HD)],
+                span_hbm.at[:, pl.ds(h * HD, HD)],
+                store_sem.at[1 + h],
             )
-            if j % 2:
-                h = 2 * i + j // 2
-                stored.append(
-                    pltpu.make_async_copy(
-                        span_out.at[:, pl.ds(h * HD, HD)],
-                        span_hbm.at[:, pl.ds(h * HD, HD)],
-                        store_sem.at[1 + h],
-                    )
-                )
-                stored[-1].start()
+        )
+        stored[-1].start()
 
     for i in range(2):
         part_copy(i).wait_send()
-        stat_copy(i).wait_send()
+    stat_copy().wait_send()
     for copy in stored:
         copy.wait()
 
@@ -669,8 +707,10 @@
         + [
             pltpu.VMEM((5, CHUNKS, 4, 2 * PIECE, 256), bf16),
             pltpu.VMEM((2, CHUNKS, 4, 2 * PIECE, 256), bf16),
-            pltpu.VMEM((2, CHUNKS, 4, PIECE, 256), bf16),
-            pltpu.VMEM((2, CHUNKS, 4, PIECE, 256), bf16),
+            pltpu.VMEM((2, 4, 2 * PIECE, 256), bf16),
+            pltpu.VMEM((2, 4, 2 * PIECE, 256), bf16),
+            pltpu.VMEM((2, 4, PIECE, 256), bf16),
+            pltpu.VMEM((2, 4, PIECE, 256), bf16),
             pltpu.VMEM((NZ, CHUNKS, 4, 2 * PIECE, 256), bf16),
             pltpu.VMEM((4, 8, 128), jnp.int32),
             pltpu.SMEM((8, 128), jnp.int32),
@@ -707,8 +747,8 @@
             dma((4,)),
             dma((2,)),
             dma((2,)),
-            dma((2,)),
-            dma((2,)),
+            dma((1,)),
+            dma((1,)),
         ],
         compiler_params=pltpu.CompilerParams(
             collective_id=0, has_side_effects=True, vmem_limit_bytes=56 * 1024 * 1024

time: 64.3 us -> 63.2 us (0.983)
  the two profiles are of different devices: /device:TPU:32 before, /device:TPU:88 now
where the time goes in v5:
time: 63.2 us; the launch traced here: 63.1 us
  Pallas kernels  62.4 us (99%)
  between operations  0.64 us (1%)
    pallas_call x1, Pallas kernels, local(): pl.pallas_call(staged, out_shape=(jax.ShapeDtypeStruct(span_query.shape,...  60.7 us
    pallas_call x1, Pallas kernels, local(): pl.pallas_call(place_results, out_shape=(jax.ShapeDtypeStruct(span_query....  1.68 us

profile of v5, /device:TPU:88, one launch (start us, length us, event | category | flops | bytes accessed | tf_op | source)
XLA Modules:
  0.0 63.1 jit_solution(7860751530949128839)
XLA Ops:
  0.6 60.7 %spanned_attention.1 = (bf16[256,512]{1,0:T(8,128)(2,1)}, bf16[32,512]{1,0:T(8,128)(2,1)}) custom-call(s32[32]{0:T(128)} %bitcast.3, s32[32]{0:T(128)} %refs_1_.1, s32[4,32]{1,0:T(4,128)} %bitcast.2, s32[1,32]{1,0:T(1,128)} %refs_3_.1, bf16[32,512]{1,0:T(8,128)(2,1)} %refs_4_.1, bf16[32,256]{1,0:T(8,128)(2,1)} %refs_5_.1, bf16[256,256]{1,0:T(8,128)(2,1)} %refs_6_.1, ...), custom_call_target="tpu_custom_call" | custom-call | flops 5000000000 | bytes 3145728 | tf_op jit(solution)/shard_map/spanned_attention/pallas_call | solution.py:685
  61.4 1.7 %place_results.1 = (bf16[256,512]{1,0:T(8,128)(2,1)}, bf16[32,512]{1,0:T(8,128)(2,1)}) custom-call(bf16[256,512]{1,0:T(8,128)(2,1)} %get-tuple-element.4.span_ref, bf16[32,512]{1,0:T(8,128)(2,1)} %get-tuple-element.5.decode_ref), custom_call_target="tpu_custom_call" | custom-call | tf_op jit(solution)/shard_map/place_results/pallas_call | solution.py:772

commit v6 on v5

--- a/solution.py
+++ b/solution.py
@@ -64,8 +64,6 @@
     near_stage,
     wide_stage,
     wide_in,
-    far_stage,
-    far_in,
     inbox,
     tabs,
     tabs_s,
@@ -454,17 +452,17 @@
 
     def far_copy(d, ch):
         return remote(
-            (wide_stage, far_stage)[ch].at[d],
-            (wide_in, far_in)[ch].at[d],
+            wide_stage.at[ch, d],
+            wide_in.at[ch, d],
             fsend.at[d, ch],
             frecv.at[d, ch],
             device(0, up_down[d]),
         )
 
     def last_copy(d, ch, e):
-        place = inbox.at[4, ch, e] if ch == 0 else inbox.at[4, ch, e, pl.ds(d * PIECE, PIECE)]
+        place = inbox.at[4, ch, e]
         return remote(
-            (wide_in, far_in)[ch].at[d, e],
+            wide_in.at[ch, d, e],
             place,
             gsend.at[d, ch, e],
             grecv.at[d, ch, e],
@@ -476,10 +474,7 @@
         return (first < 4) if d == 0 else (first >= 4)
 
     def if_used(d, ch, hops, do):
-        if ch == 0:
-            pl.when(on_way(d, hops))(do)
-        else:
-            do()
+        pl.when(on_way(d, hops))(do)
 
     def send_far(ch):
         for d in range(2):
@@ -489,12 +484,9 @@
 
             def send(d=d, block=block, owner=owner):
                 for e in range(4):
-                    if ch == 0:
-                        for rank in range(2):
-                            slot = asked(near_s.at[2 * d + 1], e, owner, rank)
-                            wide_stage[d, e, pl.ds(rank * PIECE, PIECE), :] = block[slot]
-                    else:
-                        far_stage[d, e] = block[asked(near_s.at[2 * d + 1], e, owner, d)]
+                    for rank in range(2):
+                        slot = asked(near_s.at[2 * d + 1], e, owner, rank)
+                        wide_stage[ch, d, e, pl.ds(rank * PIECE, PIECE), :] = block[slot]
                 far_copy(d, ch).start()
 
             if_used(d, ch, 2, send)
@@ -707,10 +699,8 @@
         + [
             pltpu.VMEM((5, CHUNKS, 4, 2 * PIECE, 256), bf16),
             pltpu.VMEM((2, CHUNKS, 4, 2 * PIECE, 256), bf16),
-            pltpu.VMEM((2, 4, 2 * PIECE, 256), bf16),
-            pltpu.VMEM((2, 4, 2 * PIECE, 256), bf16),
-            pltpu.VMEM((2, 4, PIECE, 256), bf16),
-            pltpu.VMEM((2, 4, PIECE, 256), bf16),
+            pltpu.VMEM((2, 2, 4, 2 * PIECE, 256), bf16),
+            pltpu.VMEM((2, 2, 4, 2 * PIECE, 256), bf16),
             pltpu.VMEM((NZ, CHUNKS, 4, 2 * PIECE, 256), bf16),
             pltpu.VMEM((4, 8, 128), jnp.int32),
             pltpu.SMEM((8, 128), jnp.int32),

time: 63.2 us -> 63.9 us (1.011)
  the two profiles are of different devices: /device:TPU:88 before, /device:TPU:16 now
where the time goes in v6:
time: 63.9 us; the launch traced here: 63.8 us
  Pallas kernels  63.1 us (99%)
  between operations  0.64 us (1%)
    pallas_call x1, Pallas kernels, local(): pl.pallas_call(staged, out_shape=(jax.ShapeDtypeStruct(span_query.shape,...  61.5 us
    pallas_call x1, Pallas kernels, local(): pl.pallas_call(place_results, out_shape=(jax.ShapeDtypeStruct(span_query....  1.68 us

profile of v6, /device:TPU:16, one launch (start us, length us, event | category | flops | bytes accessed | tf_op | source)
XLA Modules:
  0.0 63.8 jit_solution(14347228526085495323)
XLA Ops:
  0.6 61.5 %spanned_attention.1 = (bf16[256,512]{1,0:T(8,128)(2,1)}, bf16[32,512]{1,0:T(8,128)(2,1)}) custom-call(s32[32]{0:T(128)} %bitcast.3, s32[32]{0:T(128)} %refs_1_.1, s32[4,32]{1,0:T(4,128)} %bitcast.2, s32[1,32]{1,0:T(1,128)} %refs_3_.1, bf16[32,512]{1,0:T(8,128)(2,1)} %refs_4_.1, bf16[32,256]{1,0:T(8,128)(2,1)} %refs_5_.1, bf16[256,256]{1,0:T(8,128)(2,1)} %refs_6_.1, ...), custom_call_target="tpu_custom_call" | custom-call | flops 5000000000 | bytes 3145728 | tf_op jit(solution)/shard_map/spanned_attention/pallas_call | solution.py:677
  62.1 1.7 %place_results.1 = (bf16[256,512]{1,0:T(8,128)(2,1)}, bf16[32,512]{1,0:T(8,128)(2,1)}) custom-call(bf16[256,512]{1,0:T(8,128)(2,1)} %get-tuple-element.4.span_ref, bf16[32,512]{1,0:T(8,128)(2,1)} %get-tuple-element.5.decode_ref), custom_call_target="tpu_custom_call" | custom-call | tf_op jit(solution)/shard_map/place_results/pallas_call | solution.py:762
